TPU v7x, 128 devices: a whole 4x4x4 slice. The times are simulated.
128 devices in a mesh: gx: 8 (over x, z_hi), gy: 16 (over z_lo, y, core).
Axes of the slice: x: 4, y: 4, z: 4 (z_hi: 2, z_lo: 2; z = z_hi * 2 + z_lo), core: 2. Of those that a mesh axis runs over, the one named last changes fastest.
Arguments:
- density: bfloat16 [4, 64, 16384], P(None, 'gx', 'gy'), may hold values from -6 to 6
- weight_one: bfloat16 [64, 108], replicated, may hold values from -0.625 to 0.625
- weight_two: bfloat16 [256, 1728], P('gx'), may hold values from -0.15625 to 0.15625
- feature_cot: bfloat16 [256, 32, 4096], P('gx', 'gy'), may hold values from -0.0390625 to 0.0390625
Outputs:
- features: bfloat16 [256, 32, 4096], P('gx', 'gy')
- grad_one: float32 [64, 108], replicated
- grad_two: float32 [256, 1728], P('gx')
All inputs are finite; a program needn't handle non-finite values.
Results may differ from a plain program's by a relative error of at most 0.025.
Values may be sent and summed in bfloat16 or wider, within the bound.
No kernel may reach another device: no remote copies, remote signals or barrier semaphores. Data moves between devices by JAX's collectives and lax.ppermute only.
A program may use at most 128 MiB of HBM per device.

v0:
```python
import jax
import jax.numpy as jnp
from jax import lax
from jax.sharding import PartitionSpec as P

C1 = 64
Z = 64


def padded_2(cells, sides, width):
    for axis, dim in sides:
        count = lax.axis_size(axis)
        head = lax.slice_in_dim(cells, 0, width, axis=dim)
        tail = lax.slice_in_dim(cells, cells.shape[dim] - width, cells.shape[dim], axis=dim)
        cells = jnp.concatenate(
            [
                lax.ppermute(tail, axis, [(i, (i + 1) % count) for i in range(count)]),
                cells,
                lax.ppermute(head, axis, [((i + 1) % count, i) for i in range(count)]),
            ],
            axis=dim,
        )
    return cells


def leaky_relu(values):
    return values * (0.65 + 0.35 * jnp.tanh(values))


def relu_slope(values):
    bent = jnp.tanh(values)
    return (0.65 + 0.35 * bent + 0.35 * values * (1.0 - bent * bent)).astype(jnp.float32)


def kernel_of(weight, inputs):
    outputs = weight.shape[0]
    return weight.reshape(outputs, 3, 3, 3, inputs).transpose(0, 4, 1, 2, 3)


def flipped(kernel):
    return jnp.flip(kernel, (2, 3, 4)).transpose(1, 0, 2, 3, 4)


def pad_depth(values):
    return jnp.pad(values, ((0, 0), (0, 0), (0, 0), (1, 1)))


def pad_rows(values):
    return jnp.pad(values, ((0, 0), (0, 0), (1, 1), (0, 0)), mode="wrap")


def conv_valid(padded, kernel):
    result = lax.conv_general_dilated(
        padded[None],
        kernel,
        (1, 1, 1),
        "VALID",
        dimension_numbers=("NCDHW", "OIDHW", "NCDHW"),
        preferred_element_type=jnp.float32,
    )
    return result[0]


def tap_grads(padded, grad_cells):
    outputs, size_x, size_y, size_z = grad_cells.shape
    pieces = []
    for step_x in range(3):
        for step_y in range(3):
            for step_z in range(3):
                window = padded[
                    :, step_x : step_x + size_x, step_y : step_y + size_y, step_z : step_z + size_z
                ]
                pieces.append(
                    jnp.einsum(
                        "oxyz,ixyz->oi", grad_cells, window, preferred_element_type=jnp.float32
                    )
                )
    stacked = jnp.stack(pieces, axis=1)
    return stacked.reshape(outputs, -1)


def body(density, weight_one, weight_two, feature_cot):
    channels_in = density.shape[0]
    rows_x = density.shape[1]
    rows_y = density.shape[2] // Z
    volume = density.reshape(channels_in, rows_x, rows_y, Z)
    framed = padded_2(volume, (("gx", 1), ("gy", 2)), 1)
    padded_one = pad_depth(framed)
    pre_one = conv_valid(padded_one, kernel_of(weight_one, channels_in))
    act_one = leaky_relu(pre_one)
    half_x = rows_x // 2
    half_y = rows_y // 2
    half_z = Z // 2
    pooled = (
        act_one.reshape(C1, half_x, 2, half_y, 2, half_z, 2)
        .mean(axis=(2, 4, 6))
        .astype(jnp.bfloat16)
    )
    pooled_flat = pooled.reshape(C1, half_x, half_y * half_z)
    gathered = lax.all_gather(pooled_flat, "gx", axis=1, tiled=True)
    strip = lax.all_to_all(gathered, "gy", split_axis=1, concat_axis=2, tiled=True)
    strip_x = strip.shape[1]
    all_y = strip.shape[2] // half_z
    framed_two = padded_2(strip, (("gy", 1),), 1)
    padded_two = pad_depth(pad_rows(framed_two.reshape(C1, strip_x + 2, all_y, half_z)))
    kernel_two = kernel_of(weight_two, C1)
    pre_two = conv_valid(padded_two, kernel_two)
    filters_here = pre_two.shape[0]
    features = (
        leaky_relu(pre_two).astype(jnp.bfloat16).reshape(filters_here, strip_x, all_y * half_z)
    )
    cotangent = feature_cot.reshape(pre_two.shape).astype(jnp.float32)
    grads_two = (cotangent * relu_slope(pre_two)).astype(jnp.bfloat16)
    grad_two = lax.psum(tap_grads(padded_two, grads_two).astype(jnp.bfloat16), "gy").astype(
        jnp.float32
    )
    rimmed = padded_2(grads_two.reshape(filters_here, strip_x, all_y * half_z), (("gy", 1),), 1)
    padded_back = pad_depth(pad_rows(rimmed.reshape(filters_here, strip_x + 2, all_y, half_z)))
    partial_value = conv_valid(padded_back, flipped(kernel_two))
    returned = lax.all_to_all(
        partial_value.reshape(C1, strip_x, all_y * half_z).astype(jnp.bfloat16),
        "gy",
        split_axis=2,
        concat_axis=1,
        tiled=True,
    )
    summed = lax.psum_scatter(returned, "gx", scatter_dimension=1, tiled=True).astype(jnp.float32)
    pooled_grad = summed.astype(jnp.bfloat16).reshape(C1, half_x, half_y, half_z)
    grown = jnp.repeat(jnp.repeat(jnp.repeat(pooled_grad, 2, 1), 2, 2), 2, 3)
    grads_one = (grown.astype(jnp.float32) * (0.125 * relu_slope(pre_one))).astype(jnp.bfloat16)
    grad_one = lax.psum(tap_grads(padded_one, grads_one), ("gx", "gy"))
    return (features, grad_one, grad_two)


def solution(mesh):
    return jax.shard_map(
        body,
        mesh=mesh,
        in_specs=(P(None, "gx", "gy"), P(), P("gx", None), P("gx", "gy", None)),
        out_specs=(P("gx", "gy", None), P(), P("gx", None)),
        check_vma=False,
    )
```

profile of v0, /device:TPU:1, one launch (start us, length us, event | category | flops | bytes accessed | tf_op | source)
XLA Modules:
  0.0 647.3 jit_solution(17938824529276376677)
XLA Ops:
  8.4 4.5 collective-permute-start
  12.9 2.3 collective-permute-start.1
  17.3 1.9 collective-permute-start.3
  19.2 1.6 collective-permute-start.2
  23.4 3.9 copy.437
  27.5 13.4 %multiply_add_fusion = (f32[8,16,8,9,64]{4,2,3,1,0:T(8,128)}, f32[8,16,8,9,64]{4,2,3,1,0:T(8,128)}, f32[8,16,8,9,64]{4,2,3,1,0:T(8,128)S(1)}) fusion(bf16[64,3,3,3,4]{0,4,3,2,1:T(4,128)(2,1)S(1)} %reshape.107, bf16[4,10,18,1,7,2]{4,0,5,2,1,3:T(4,128)(2,1)S(1)} %slice.316, bf16[4,10,18,1,8,9]{4,0,5,2,1,3:T(4,128)(2,1)S(1)} %copy.437, ...), kind=kOutput, calls=%fused_computation.20 | convolution fusion | flops 131910912 | bytes 7215624 | tf_op jit(solution)/shard_map/conv_general_dilated | solution.py:53
  42.1 4.7 multiply_reduce_fusion
  47.8 48.7 %all-gather.2.cloned.1.call-done = bf16[64,32,256]{2,0,1:T(8,128)(2,1)} async-done(((bf16[64,4,256]{2,0,1:T(8,128)(2,1)}), bf16[64,32,256]{2,0,1:T(8,128)(2,1)}) %all-gather.2.cloned.1.call-update) | async-done | bytes 1048592 | tf_op jit(solution)/shard_map/all_gather | solution.py:100
  96.5 6.2 all-to-all-start
  102.9 15.6 %all-to-all-done = bf16[64,32,256]{2,0,1:T(8,128)(2,1)S(1)} async-done(((bf16[64,32,256]{2,0,1:T(8,128)(2,1)}), bf16[64,32,256]{2,0,1:T(8,128)(2,1)S(1)}, u32[]{:S(2)}, u32[]{:S(2)}) %all-to-all-start) | async-done | bytes 1048608 | tf_op jit(solution)/shard_map/all_to_all | solution.py:101
  121.7 2.8 reshape.142
  124.5 3.6 copy.504
  129.2 2.2 copy.447
  134.1 1.7 copy.444
  140.2 3.8 fusion.324
  144.0 3.6 pad.17
  147.6 9.7 %copy.450 = bf16[64,4,130,1,8,5]{0,4,5,2,1,3:T(8,128)(2,1)} copy(bf16[64,4,130,1,8,5]{2,0,5,4,1,3:T(8,128)(2,1)} %bitcast.720) | data formatting | bytes 5324800 | tf_op jit(solution)/shard_map/conv_general_dilated | solution.py:53
  157.2 2.2 slice.322
  159.4 23.0 %fusion.9 = f32[2,128,8,5,32]{4,2,3,1,0:T(8,128)} fusion(bf16[64,4,130,1,7,2]{0,4,5,2,1,3:T(8,128)(2,1)S(1)} %slice.322, bf16[64,4,130,1,8,5]{0,4,5,2,1,3:T(8,128)(2,1)} %copy.450, bf16[32,3,3,3,64]{4,3,2,1,0:T(4,128)(2,1)S(1)} %reshape.108), kind=kOutput, calls=%fused_computation.12 | convolution fusion | flops 1143644160 | bytes 5015552 | tf_op jit(solution)/shard_map/conv_general_dilated | solution.py:53
  182.4 5.2 copy.452
  187.7 3.3 multiply_add_fusion.1
  192.1 3.7 copy.453
  195.7 4.3 squeeze.7
  200.0 2.7 multiply_convert_fusion.1
  204.4 3.5 concatenate.74
  207.8 5.2 select_maximum_fusion
  213.2 2.1 collective-permute-start.6
  226.3 1.6 fusion.103
  234.1 3.0 copy.520
  237.0 2.1 fusion.91
  239.1 3.1 fusion.89
  242.2 2.9 fusion.87
  253.4 2.7 copy.456
  256.1 2.3 fusion.73
  258.4 1.8 concatenate.75
  260.3 1.6 copy.457
  261.8 2.7 concatenate.73
  264.6 2.2 copy.455
  272.3 2.2 pad.19
  274.5 8.9 %copy.460 = bf16[32,4,130,1,8,5]{0,4,5,2,1,3:T(8,128)(2,1)} copy(bf16[32,4,130,1,8,5]{2,0,5,4,1,3:T(8,128)(2,1)} %bitcast.729) | data formatting | bytes 2662400 | tf_op jit(solution)/shard_map/conv_general_dilated | solution.py:53
  283.4 2.2 slice.328
  285.6 12.2 %fusion.5 = bf16[2,128,8,5,64]{4,2,3,1,0:T(8,128)(2,1)} fusion(bf16[32,4,130,1,7,2]{0,4,5,2,1,3:T(8,128)(2,1)S(1)} %slice.328, bf16[32,4,130,1,8,5]{0,4,5,2,1,3:T(8,128)(2,1)} %copy.460, bf16[32,3,3,3,64]{4,3,2,1,0:T(4,128)(2,1)S(1)} %copy-done.35), kind=kOutput, calls=%fused_computation.9 | convolution fusion | flops 1138053120 | bytes 3218432 | tf_op jit(solution)/shard_map/conv_general_dilated | solution.py:53
  297.8 4.7 copy.462
  302.5 1.6 select_convert_fusion
  305.2 4.7 copy.463
  309.9 15.1 %copy.680 = bf16[64,2,4096]{0,1,2:T(2,128)(2,1)} copy(bf16[64,2,4096]{0,2,1:T(8,128)(2,1)} %bitcast.735) | data formatting | bytes 2097152 | tf_op jit(solution)/shard_map/convert_element_type | solution.py:121
  325.0 5.8 reshape.219
  330.8 6.5 all-to-all-start.1
  337.3 3.1 fusion.71
  340.5 3.0 fusion.69
  343.5 1.6 fusion.67
  345.1 2.9 fusion.65
  349.9 3.3 all-to-all-done.1
  353.2 5.0 reshape.220
  358.2 3.4 copy.596
  361.6 5.4 copy.470
  367.0 5.4 copy.469
  374.0 88.0 %all-reduce.5.cloned.1.call-done = bf16[32,1728]{1,0:T(8,128)(2,1)} async-done(((bf16[32,1728]{1,0:T(8,128)(2,1)}), bf16[32,1728]{1,0:T(8,128)(2,1)}) %all-reduce.5.cloned.1.call-update) | async-done | bytes 110608 | tf_op jit(solution)/shard_map/psum | solution.py:114
  462.0 1.6 convert_element_type.105
  463.7 75.0 %reduce-scatter.2.cloned.1.call-done = bf16[64,4,256]{2,0,1:T(8,128)(2,1)} async-done(((bf16[64,32,256]{2,0,1:T(8,128)(2,1)}), bf16[64,4,256]{2,0,1:T(8,128)(2,1)}) %reduce-scatter.2.cloned.1.call-update) | async-done | bytes 131088 | tf_op jit(solution)/shard_map/reduce_scatter | solution.py:127
  542.3 1.6 copy-done.16
  544.0 3.9 fusion.22
  547.9 3.9 copy.471
  573.3 66.6 %psum.14 = f32[64,108]{0,1:T(8,128)S(1)} all-reduce(f32[64,108]{0,1:T(8,128)S(1)} %reshape.109), channel_id=1, replica_groups=mesh['gx'=8,'gy'=16] {'gx','gy'}, use_global_device_ids=true, to_apply=%region_2.3 | all-reduce | flops 6912 | bytes 55296 | tf_op jit(solution)/shard_map/psum | solution.py:131
  (213 shorter events, 83.7 us)
Async XLA Ops:
  7.2 89.3 %all-gather.2.cloned.1.call-start = ((), (), s32[]{:S(2)}) async-start(), calls=%async_computation.3 | async-start | bytes 1179648 | tf_op jit(solution)/shard_map/all_gather | solution.py:100
  8.2 13.8 %copy-start.32 = (bf16[4,8,16,64]{3,2,1,0:T(8,128)(2,1)}, bf16[4,8,16,64]{3,2,1,0:T(8,128)(2,1)S(1)}, u32[]{:S(2)}) copy-start(bf16[4,8,16,64]{3,2,1,0:T(8,128)(2,1)S(1)} %reshape.106) | copy-start | bytes 196612
  8.3 8.9 %copy-start.30 = (bf16[4,8,16,64]{3,0,2,1:T(4,128)(2,1)}, bf16[4,8,16,64]{3,0,2,1:T(4,128)(2,1)S(1)}, u32[]{:S(2)}) copy-start(bf16[4,8,16,64]{3,0,2,1:T(4,128)(2,1)S(1)} %copy.432) | copy-start | bytes 196612
  8.4 7.8 %collective-permute-start = (bf16[4,1,16,64]{3,0,2,1:T(4,128)(2,1)S(1)}, bf16[4,1,16,64]{3,0,2,1:T(4,128)(2,1)S(1)}, u32[]{:S(2)}, u32[]{:S(2)}) collective-permute-start(bf16[4,1,16,64]{3,0,2,1:T(4,128)(2,1)S(1)} %get-tuple-element.40), channel_id=1, source_target_pairs={{0,16},{16,32},{32,48},{48,64},{64,80},{80,96},{96,112},{112,0},{1... | collective-permute-start | bytes 24584 | tf_op jit(solution)/shard_map/ppermute | solution.py:17
  12.9 4.4 collective-permute-start.1
  16.2 3.0 copy-start.43
  17.3 1.9 copy-start.41
  17.3 10.0 %copy-start.18 = (bf16[4,10,16,64]{3,0,2,1:T(4,128)(2,1)}, bf16[4,10,16,64]{3,0,2,1:T(4,128)(2,1)S(1)}, u32[]{:S(2)}) copy-start(bf16[4,10,16,64]{3,0,2,1:T(4,128)(2,1)S(1)} %constant_dynamic-update-slice_fusion) | copy-start | bytes 245764
  17.3 4.4 collective-permute-start.3
  19.2 2.5 collective-permute-start.2
  21.7 0.6 copy-start.36
  21.7 0.6 copy-start.38
  23.0 4.6 copy-start.46
  46.9 55.9 %copy-start.40 = (bf16[32,1728]{1,0:T(8,128)(2,1)S(1)}, bf16[32,1728]{1,0:T(8,128)(2,1)}, u32[]{:S(2)}) copy-start(bf16[32,1728]{1,0:T(8,128)(2,1)} %param.6) | copy-start | bytes 331780
  96.5 22.0 %all-to-all-start = ((bf16[64,32,256]{2,0,1:T(8,128)(2,1)}), bf16[64,32,256]{2,0,1:T(8,128)(2,1)S(1)}, u32[]{:S(2)}, u32[]{:S(2)}) async-start(bf16[64,32,256]{2,0,1:T(8,128)(2,1)} %all-gather.2.cloned.1.call-done), calls=%async_computation | async-start | bytes 2097152 | tf_op jit(solution)/shard_map/all_to_all | solution.py:101
  102.9 56.5 %copy-start.34 = (bf16[32,3,3,3,64]{4,3,2,1,0:T(4,128)(2,1)}, bf16[32,3,3,3,64]{4,3,2,1,0:T(4,128)(2,1)S(1)}, u32[]{:S(2)}) copy-start(bf16[32,3,3,3,64]{4,3,2,1,0:T(4,128)(2,1)S(1)} %reshape.108) | copy-start | bytes 331780
  118.5 2.9 copy-start.28
  119.7 11.7 %collective-permute-start.5 = (bf16[64,1,4096]{2,0,1:T(8,128)(2,1)}, bf16[64,1,4096]{2,0,1:T(8,128)(2,1)}, u32[]{:S(2)}, u32[]{:S(2)}) collective-permute-start(bf16[64,1,4096]{2,0,1:T(8,128)(2,1)} %get-tuple-element.32), channel_id=1, source_target_pairs={{1,0},{2,1},{3,2},{4,3},{5,4},{6,5},{7,6},{8,7},{9,8},{10,9},{11,1... | collective-permute-start | bytes 1572872 | tf_op jit(solution)/shard_map/ppermute | solution.py:19
  120.4 13.7 %collective-permute-start.4 = (bf16[64,1,4096]{2,0,1:T(8,128)(2,1)}, bf16[64,1,4096]{2,0,1:T(8,128)(2,1)}, u32[]{:S(2)}, u32[]{:S(2)}) collective-permute-start(bf16[64,1,4096]{2,0,1:T(8,128)(2,1)} %get-tuple-element.31), channel_id=1, source_target_pairs={{0,1},{1,2},{2,3},{3,4},{4,5},{5,6},{6,7},{7,8},{8,9},{9,10},{10,1... | collective-permute-start | bytes 1572872 | tf_op jit(solution)/shard_map/ppermute | solution.py:17
  134.0 2.9 copy-start.3
  136.9 0.8 copy-start.8
  137.9 2.2 copy-start.4
  137.9 2.2 copy-start.9
  138.8 1.3 copy-start
  182.4 5.2 copy-start.45
  202.7 0.8 copy-start.20
  207.8 7.4 %copy-start.25 = (f32[2,128,8,5,32]{1,4,3,2,0:T(8,128)S(1)}, f32[2,128,8,5,32]{1,4,3,2,0:T(8,128)}, u32[]{:S(2)}) copy-start(f32[2,128,8,5,32]{1,4,3,2,0:T(8,128)} %get-tuple-element.25) | copy-start | bytes 3932164
  213.1 19.7 %copy-start.22 = (bf16[64,4,130,34]{2,0,3,1:T(8,128)(2,1)}, bf16[64,4,130,34]{2,0,3,1:T(8,128)(2,1)S(1)}, u32[]{:S(2)}) copy-start(bf16[64,4,130,34]{2,0,3,1:T(8,128)(2,1)S(1)} %select_maximum_fusion) | copy-start | bytes 6789124
  213.1 2.3 copy-start.24
  213.1 45.3 %collective-permute-start.7 = (bf16[32,1,4096]{2,0,1:T(8,128)(2,1)}, bf16[32,1,4096]{2,0,1:T(8,128)(2,1)S(1)}, u32[]{:S(2)}, u32[]{:S(2)}) collective-permute-start(bf16[32,1,4096]{2,0,1:T(8,128)(2,1)} %get-tuple-element.36), channel_id=1, source_target_pairs={{1,0},{2,1},{3,2},{4,3},{5,4},{6,5},{7,6},{8,7},{9,8},{10,9},{11,1... | collective-permute-start | bytes 786440 | tf_op jit(solution)/shard_map/ppermute | solution.py:19
  213.2 48.7 %collective-permute-start.6 = (bf16[32,1,4096]{2,0,1:T(8,128)(2,1)}, bf16[32,1,4096]{2,0,1:T(8,128)(2,1)}, u32[]{:S(2)}, u32[]{:S(2)}) collective-permute-start(bf16[32,1,4096]{2,0,1:T(8,128)(2,1)} %get-tuple-element.35), channel_id=1, source_target_pairs={{0,1},{1,2},{2,3},{3,4},{4,5},{5,6},{6,7},{7,8},{8,9},{9,10},{10,1... | collective-permute-start | bytes 786440 | tf_op jit(solution)/shard_map/ppermute | solution.py:17
  215.3 1.2 copy-start.26
  216.5 2.3 copy-start.1
  216.5 2.3 copy-start.5
  216.5 2.3 copy-start.10
  217.7 15.1 %copy-start.13 = (bf16[32,2,128,32]{2,3,1,0:T(8,128)(2,1)}, bf16[32,2,128,32]{2,3,1,0:T(8,128)(2,1)S(1)}, u32[]{:S(2)}) copy-start(bf16[32,2,128,32]{2,3,1,0:T(8,128)(2,1)S(1)} %fusion.202) | copy-start | bytes 1572868
  237.0 5.2 copy-start.14
  239.1 6.0 copy-start.6
  239.1 6.0 copy-start.11
  245.1 2.3 copy-start.23
  247.4 2.3 copy-start.2
  268.0 1.0 copy-start.21
  268.0 1.1 copy-start.27
  283.4 2.2 copy-start.35
  330.8 22.4 %all-to-all-start.1 = ((bf16[16,2,16384]{2,1,0:T(2,128)(2,1)}), bf16[16,2,16384]{2,1,0:T(2,128)(2,1)}, u32[]{:S(2)}, u32[]{:S(2)}) async-start(bf16[16,2,16384]{2,1,0:T(2,128)(2,1)} %reshape.219), calls=%async_computation.1 | async-start | bytes 2097152 | tf_op jit(solution)/shard_map/all_to_all | solution.py:120
  337.3 124.8 %all-reduce.5.cloned.1.call-start = ((), (), s32[]{:S(2)}) async-start(), calls=%async_computation.5 | async-start | bytes 229376 | tf_op jit(solution)/shard_map/psum | solution.py:114
  337.3 6.2 copy-start.7
  337.3 6.2 copy-start.12
  337.3 6.2 copy-start.15
  349.9 188.8 %reduce-scatter.2.cloned.1.call-start = ((), (), s32[]{:S(2)}) async-start(), calls=%async_computation.4 | async-start | bytes 1179648 | tf_op jit(solution)/shard_map/reduce_scatter | solution.py:127
  367.0 5.4 copy-start.19
  367.0 5.4 copy-start.37
  367.0 5.4 copy-start.39
  367.0 5.7 copy-start.29
  538.6 2.6 slice-start
  540.1 2.2 slice-start.1
  540.9 3.1 copy-start.16
  553.1 1.4 copy-start.31
  553.1 1.4 copy-start.44
  560.7 2.2 copy-start.17
  562.9 0.9 copy-start.33
  568.4 1.4 copy-start.42
Sparse Core Ops, SparseCore 0:
  47.9 48.5 all-gather.1
  350.0 112.0 all-reduce.4
  466.1 72.4 reduce-scatter.1
where the time goes:
time: 658 us; the launch traced here: 647 us
  waiting for transfers between devices  233 us (35%)
  local copies, waits for them, and re-layouts  162 us (25%)
  matrix products  112 us (17%)
  blocking collectives  66.6 us (10%)
  other arithmetic  32.8 us (5%)
  starting transfers between devices  27 us (4%)
  between operations  14.7 us (2%)
    psum x1, waiting for transfers between devices, body(): lax.psum(tap_grads(padded_two, grads_two).astype(jnp.bfloat16), 'gy')  88 us
    reduce_scatter x1, waiting for transfers between devices, body(): lax.psum_scatter(returned, 'gx', scatter_dimension=1, tiled=True)  75 us
    psum x1, blocking collectives, body(): grad_one = lax.psum(tap_grads(padded_one, grads_one), ('gx', 'gy'))  66.6 us
    dot_general x54, matrix products, tap_grads(): jnp.einsum('oxyz,ixyz->oi', grad_cells, window, preferred_element_type=jn...  63.1 us
    all_gather x1, waiting for transfers between devices, body(): gathered = lax.all_gather(pooled_flat, 'gx', axis=1, tiled=True)  48.7 us
    conv_general_dilated x3, matrix products, conv_valid(): lax.conv_general_dilated(padded[None], kernel, (1, 1, 1), 'VALID', dimens...  48.6 us
    conv_general_dilated x12, local copies, waits for them, and re-layouts, conv_valid(): lax.conv_general_dilated(padded[None], kernel, (1, 1, 1), 'VALID', dimens...  43 us
    unnamed x106, local copies, waits for them, and re-layouts  24.3 us
  transfers between devices with their start and end apart: 13, of which 7 were waited for; matrix products, arithmetic and copies ran while one was open for 14% of the time, Pallas kernels for 0%

commit v1 on v0

v1 whole, which is shorter than its diff:
```python
import jax
import jax.numpy as jnp
import numpy as np
from jax import lax
from jax.experimental import pallas as pl
from jax.experimental.pallas import tpu as pltpu
from jax.sharding import PartitionSpec as P

C0 = 4
C1 = 64
Z = 64
HZ = 32
CELLS = 4096
ROWS = 4
TILE = 512
F32 = jnp.float32
BF16 = jnp.bfloat16


def split_depth():
    sort = np.zeros((1024, 1024), np.float32)
    for y in range(16):
        for z in range(Z):
            sort[y * Z + z, ((y % 2) * 2 + z % 2) * 256 + (y // 2) * HZ + z // 2] = 1
    return sort


def window_taps():
    place = {(1, 1): 0, (0, 0): 1, (0, 1): 2, (1, 0): 3}
    taps = np.zeros((8, 256, 128), np.float32)
    for cell in range(8):
        a, b, c = cell // 4, cell // 2 % 2, cell % 2
        for x in range(4):
            for y_key, y in place.items():
                for z_key, z in place.items():
                    dx, dy, dz = x - a, y - b, z - c
                    if min(dx, dy, dz) < 0 or max(dx, dy, dz) > 2:
                        continue
                    row = x * 64 + y_key[0] * 32 + z_key[0] * 16 + y_key[1] * 8 + z_key[1] * 4
                    for i in range(C0):
                        taps[cell, row + i, (9 * dx + 3 * dy + dz) * C0 + i] = 1
    return taps


def depth_of(shape):
    return lax.broadcasted_iota(jnp.int32, shape, 1) % HZ


def move(values, step):
    return pltpu.roll(values, step % values.shape[1], 1)


def from_below(values, depth):
    return jnp.where(depth != 0, move(values, 1), 0.0)


def from_above(values, depth):
    return jnp.where(depth != HZ - 1, move(values, -1), 0.0)


def fine_kernel(parts_ref, weight_ref, windows_ref, pooled_ref, slope_ref):
    row, tile = pl.program_id(0), pl.program_id(1)

    @pl.when((row == 0) & (tile == 0))
    def _():
        depth = depth_of((8, CELLS))
        low = lax.broadcasted_iota(jnp.int32, (8, CELLS), 0) < 4
        for x in range(10):
            cells = jnp.concatenate(
                [parts_ref[c, 16 * x : 16 * x + 16, :] for c in range(8)], axis=1
            ).astype(F32)
            even, odd = cells[:8], cells[8:]
            for shifted, (top, bottom) in enumerate(
                ((even, odd), (move(even, -HZ), move(odd, HZ)))
            ):
                at = 64 * x + 32 * shifted
                windows_ref[at : at + 16, :] = jnp.concatenate([top, bottom], axis=0).astype(BF16)
                moved = [
                    jnp.where(low, from_above(half, depth), from_below(half, depth))
                    for half in (top, bottom)
                ]
                windows_ref[at + 16 : at + 32, :] = jnp.concatenate(moved, axis=0).astype(BF16)

    lanes = pl.ds(pl.multiple_of(tile * TILE, TILE), TILE)
    window = windows_ref[pl.ds(pl.multiple_of(row * 128, 128), 256), lanes]
    pre = jnp.dot(weight_ref[...], window, preferred_element_type=F32)
    total = None
    for cell in range(8):
        value = pre[C1 * cell : C1 * cell + C1].astype(BF16)
        bent = jnp.tanh(value)
        gate = bent * 0.35 + 0.65
        act = value * gate
        slope_ref[0, C1 * cell : C1 * cell + C1, :] = gate + (value * 0.35) * (1.0 - bent * bent)
        total = act.astype(F32) if total is None else total + act.astype(F32)
    pooled_ref[...] = (total * 0.125).astype(BF16)


def coarse_kernel(pooled_ref, forward_ref, backward_ref, cot_ref, feature_ref, back_ref, grad_ref, wide_ref, moved_ref):
    for tile in range(CELLS // TILE):
        lanes = slice(tile * TILE, tile * TILE + TILE)
        wide_ref[:, lanes] = jnp.dot(forward_ref[...], pooled_ref[:, lanes], preferred_element_type=F32)
    depth = depth_of((16, CELLS))
    for block in range(4):
        def term(dy, dz):
            at = 64 * (3 * dy + dz) + 16 * block
            return wide_ref[at : at + 16, :]

        def column(dz):
            return term(1, dz) + move(term(0, dz), HZ) + move(term(2, dz), -HZ)

        pre = column(1) + from_below(column(0), depth) + from_above(column(2), depth)
        rows = slice(16 * block, 16 * block + 16)
        bent = jnp.tanh(pre)
        gate = 0.65 + 0.35 * bent
        feature_ref[rows, :] = (pre * gate).astype(BF16)
        slope = gate + 0.35 * pre * (1.0 - bent * bent)
        grads = (cot_ref[rows, :].astype(F32) * slope).astype(BF16).astype(F32)
        for dy in range(3):
            here = grads if dy == 1 else move(grads, HZ * (dy - 1))
            for dz in range(3):
                there = here if dz == 1 else (from_above if dz == 0 else from_below)(here, depth)
                at = 64 * (3 * dy + dz) + 16 * block
                moved_ref[at : at + 16, :] = there.astype(BF16)
    for tile in range(CELLS // TILE):
        lanes = slice(tile * TILE, tile * TILE + TILE)
        back_ref[:, lanes] = jnp.dot(
            backward_ref[...], moved_ref[:, lanes], preferred_element_type=F32
        ).astype(BF16)
    grad = lax.dot_general(
        moved_ref[...], pooled_ref[...], (((1,), (1,)), ((), ())), preferred_element_type=F32
    )
    for tap in range(9):
        both = grad[64 * tap : 64 * tap + 32, :192] + grad[64 * tap + 32 : 64 * tap + 64, 64:]
        for dx in range(3):
            at = dx * 576 + tap * 64
            grad_ref[:, at : at + 64] = both[:, 64 * dx : 64 * dx + 64].astype(BF16)


def fine_back_kernel(windows_ref, slope_ref, back_ref, taps_ref, grad_ref, sum_ref):
    row, tile = pl.program_id(0), pl.program_id(1)
    lanes = pl.ds(pl.multiple_of(tile * TILE, TILE), TILE)
    window = windows_ref[pl.ds(pl.multiple_of(row * 128, 128), 256), lanes]
    back = back_ref[...]
    grads = jnp.concatenate(
        [slope_ref[0, C1 * cell : C1 * cell + C1, :] * back for cell in range(8)], axis=0
    )
    term = lax.dot_general(grads, window, (((1,), (1,)), ((), ())), preferred_element_type=F32)
    first = (row == 0) & (tile == 0)

    @pl.when(first)
    def _():
        sum_ref[...] = term

    @pl.when(jnp.logical_not(first))
    def _():
        sum_ref[...] += term

    @pl.when((row == ROWS - 1) & (tile == CELLS // TILE - 1))
    def _():
        total = jnp.zeros((C1, 128), F32)
        for cell in range(8):
            whole = sum_ref[C1 * cell : C1 * cell + C1, :]
            high = whole.astype(BF16)
            low = (whole - high.astype(F32)).astype(BF16)
            total += jnp.dot(high, taps_ref[cell], preferred_element_type=F32)
            total += jnp.dot(low, taps_ref[cell], preferred_element_type=F32)
        grad_ref[...] = total * 0.125


def fine_forward(parts, weight):
    return pl.pallas_call(
        fine_kernel,
        grid=(ROWS, CELLS // TILE),
        in_specs=[
            pl.BlockSpec((8, 160, 512), lambda r, t: (0, 0, 0)),
            pl.BlockSpec((512, 256), lambda r, t: (0, 0)),
        ],
        out_specs=[
            pl.BlockSpec((640, CELLS), lambda r, t: (0, 0)),
            pl.BlockSpec((C1, TILE), lambda r, t: (r, t)),
            pl.BlockSpec((1, 512, TILE), lambda r, t: (r, 0, t)),
        ],
        out_shape=[
            jax.ShapeDtypeStruct((640, CELLS), BF16),
            jax.ShapeDtypeStruct((ROWS * C1, CELLS), BF16),
            jax.ShapeDtypeStruct((ROWS, 512, CELLS), BF16),
        ],
        compiler_params=pltpu.CompilerParams(vmem_limit_bytes=40 << 20),
        name="fine_forward",
    )(parts, weight)


def coarse(pooled, forward, backward, cot):
    whole = pl.BlockSpec(memory_space=pltpu.VMEM)
    return pl.pallas_call(
        coarse_kernel,
        in_specs=[whole] * 4,
        out_specs=[whole] * 3,
        out_shape=[
            jax.ShapeDtypeStruct((64, CELLS), BF16),
            jax.ShapeDtypeStruct((256, CELLS), BF16),
            jax.ShapeDtypeStruct((32, 1728), BF16),
        ],
        scratch_shapes=[pltpu.VMEM((576, CELLS), F32), pltpu.VMEM((576, CELLS), BF16)],
        compiler_params=pltpu.CompilerParams(vmem_limit_bytes=48 << 20),
        name="coarse",
    )(pooled, forward, backward, cot)


def fine_backward(windows, slope, back, taps):
    return pl.pallas_call(
        fine_back_kernel,
        grid=(ROWS, CELLS // TILE),
        in_specs=[
            pl.BlockSpec((640, CELLS), lambda r, t: (0, 0)),
            pl.BlockSpec((1, 512, TILE), lambda r, t: (r, 0, t)),
            pl.BlockSpec((C1, TILE), lambda r, t: (r, t)),
            pl.BlockSpec((8, 256, 128), lambda r, t: (0, 0, 0)),
        ],
        out_specs=pl.BlockSpec((C1, 128), lambda r, t: (0, 0)),
        out_shape=jax.ShapeDtypeStruct((C1, 128), F32),
        scratch_shapes=[pltpu.VMEM((512, 256), F32)],
        compiler_params=pltpu.CompilerParams(vmem_limit_bytes=40 << 20),
        name="fine_backward",
    )(windows, slope, back, taps)


def strip_part(density):
    sort = jnp.asarray(split_depth(), BF16)
    sorted_cells = jnp.dot(density.reshape(32, 1024), sort, preferred_element_type=F32).astype(BF16)
    block = sorted_cells.reshape(C0, 8, 4, 256).transpose(1, 2, 0, 3).reshape(8, 16, 256)
    side = lax.axis_index("gy") % 2
    both = [(gx, gy) for gx in range(8) for gy in range(16)]

    def send(values, target):
        pairs = []
        for gx, gy in both:
            to_x, to_y = target(gx, gy)
            pairs.append((gx * 16 + gy, to_x * 16 + to_y % 16))
        return lax.ppermute(values, ("gx", "gy"), pairs)

    main = [block[0:7], block[1:8]]
    rim = [block[5:8], block[0:3]]
    even = side == 0
    same = send(jnp.where(even, main[0], main[1]), lambda gx, gy: (gy // 2, 2 * gx + gy % 2))
    other = send(jnp.where(even, main[1], main[0]), lambda gx, gy: (gy // 2, 2 * gx + 1 - gy % 2))
    rim_same = send(
        jnp.where(even, rim[0], rim[1]),
        lambda gx, gy: (gy // 2, 2 * gx + 2 if gy % 2 == 0 else 2 * gx - 1),
    )
    rim_other = send(
        jnp.where(even, rim[1], rim[0]),
        lambda gx, gy: (gy // 2, 2 * gx - 1 if gy % 2 == 0 else 2 * gx + 2),
    )
    lower = jnp.concatenate(
        [jnp.concatenate([rim_same, same], 0), jnp.concatenate([rim_other, other], 0)], 2
    )
    upper = jnp.concatenate(
        [jnp.concatenate([other, rim_other], 0), jnp.concatenate([same, rim_same], 0)], 2
    )
    return jnp.where(even, lower, upper).reshape(160, 512)


def coarse_weights(weight_two):
    taps = weight_two.reshape(32, 3, 9, C1)
    both = jnp.stack([jnp.pad(taps, ((0, 0), (r, 1 - r), (0, 0), (0, 0))) for r in range(2)])
    forward = both.transpose(3, 0, 1, 2, 4).reshape(576, 256)
    return forward, forward.T


def body(density, weight_one, weight_two, feature_cot):
    taps = jnp.asarray(window_taps(), BF16)
    with jax.named_scope("strip"):
        part = strip_part(density)
        parts = lax.all_to_all(jnp.broadcast_to(part[None], (8, 160, 512)), "gx", 0, 0)
    with jax.named_scope("weights"):
        fine_weight = jnp.einsum(
            "ok,srk->sor", jnp.pad(weight_one, ((0, 0), (0, 20))), taps, preferred_element_type=F32
        ).astype(BF16).reshape(512, 256)
        forward, backward = coarse_weights(weight_two)
        cot = feature_cot.transpose(1, 0, 2).reshape(64, CELLS)
    windows, pooled, slope = fine_forward(parts, fine_weight)
    features, back, grad_two = coarse(pooled, forward, backward, cot)
    features = features.reshape(2, 32, CELLS).transpose(1, 0, 2)
    with jax.named_scope("sum_two"):
        terms = lax.all_to_all(grad_two.reshape(16, 2, 1728), "gy", 0, 0)
        mine = terms.astype(F32).sum(0).astype(BF16)
        grad_two = lax.all_to_all(jnp.broadcast_to(mine[None], (16, 2, 1728)), "gy", 0, 0)
        grad_two = grad_two.reshape(32, 1728).astype(F32)
    grad_one = fine_backward(windows, slope, back, taps)
    with jax.named_scope("sum_one"):
        terms = lax.all_to_all(grad_one.reshape(16, 4, 128), "gy", 0, 0)
        mine = terms.sum(0)
        whole = lax.all_to_all(jnp.broadcast_to(mine[None], (128, 4, 128)), ("gx", "gy"), 0, 0)
        grad_one = whole.reshape(8, 64, 128).sum(0)[:, :108]
    return features, grad_one, grad_two


def solution(mesh):
    return jax.shard_map(
        body,
        mesh=mesh,
        in_specs=(P(None, "gx", "gy"), P(), P("gx", None), P("gx", "gy", None)),
        out_specs=(P("gx", "gy", None), P(), P("gx", None)),
        check_vma=False,
    )
```

time: 658 us -> 161 us (0.24); the launches traced: 647 us -> 160 us
  waiting for transfers between devices: 233 us -> 41.5 us
  local copies, waits for them, and re-layouts: 162 us -> 16.7 us
  matrix products: 112 us -> 2.35 us
  blocking collectives: 66.6 us -> 0 us
  Pallas kernels: 0 us -> 56.3 us
  other arithmetic: 32.8 us -> 1.04 us
  starting transfers between devices: 27 us -> 41.4 us
  between operations: 14.7 us -> 0.86 us
    psum x1 -> x0, waiting for transfers between devices: 88 us -> none  [body(): lax.psum(tap_grads(padded_two, grads_two).astype(jnp.bfloat16), 'gy')]
    reduce_scatter x1 -> x0, waiting for transfers between devices: 75 us -> none  [body(): lax.psum_scatter(returned, 'gx', scatter_dimension=1, tiled=True)]
    psum x1 -> x0, blocking collectives: 66.6 us -> none  [body(): grad_one = lax.psum(tap_grads(padded_one, grads_one), ('gx', 'gy'))]
    dot_general x54 -> x2, matrix products: 63.1 us -> 2.35 us  [the longest x1 2.05 us: strip_part(): jnp.dot(density.reshape(32, 1024), sort, preferred_element_type=F32)]
    pallas_call x0 -> x3, Pallas kernels: none -> 56.3 us  [the longest x1 24.9 us: fine_backward(): pl.pallas_call(fine_back_kernel, grid=(ROWS, CELLS // TILE), in_specs=[pl...]
    all_gather x1 -> x0, waiting for transfers between devices: 48.7 us -> none  [body(): gathered = lax.all_gather(pooled_flat, 'gx', axis=1, tiled=True)]
    conv_general_dilated x3 -> x0, matrix products: 48.6 us -> none  [conv_valid(): lax.conv_general_dilated(padded[None], kernel, (1, 1, 1), 'VALID', dimens...]
    conv_general_dilated x12 -> x0, local copies, waits for them, and re-layouts: 43 us -> none  [conv_valid(): lax.conv_general_dilated(padded[None], kernel, (1, 1, 1), 'VALID', dimens...]
  transfers between devices with their start and end apart: 13 -> 9, of which waited for: 7 -> 6; matrix products, arithmetic and copies ran while one was open for 14% -> 3% of each run, Pallas kernels for 0% -> 16%
where the time goes in v1:
time: 161 us; the launch traced here: 160 us
  Pallas kernels  56.3 us (35%)
  waiting for transfers between devices  41.5 us (26%)
  starting transfers between devices  41.4 us (26%)
  local copies, waits for them, and re-layouts  16.7 us (10%)
  matrix products  2.35 us (1%)
    pallas_call x1, Pallas kernels, fine_backward(): pl.pallas_call(fine_back_kernel, grid=(ROWS, CELLS // TILE), in_specs=[pl...  24.9 us
    pallas_call x1, Pallas kernels, fine_forward(): pl.pallas_call(fine_kernel, grid=(ROWS, CELLS // TILE), in_specs=[pl.Bloc...  23.7 us
    all_to_all x1, waiting for transfers between devices, body(): lax.all_to_all(jnp.broadcast_to(part[None], (8, 160, 512)), 'gx', 0, 0)  16.9 us
    all_to_all x1, starting transfers between devices, body(): lax.all_to_all(jnp.broadcast_to(part[None], (8, 160, 512)), 'gx', 0, 0)  12.1 us
    ppermute x4, starting transfers between devices, send(): return lax.ppermute(values, ('gx', 'gy'), pairs)  11.1 us
    all_to_all x1, waiting for transfers between devices, body(): lax.all_to_all(jnp.broadcast_to(mine[None], (128, 4, 128)), ('gx', 'gy'),...  8.7 us
    unnamed x17, local copies, waits for them, and re-layouts  8.63 us
    pallas_call x1, Pallas kernels, coarse(): pl.pallas_call(coarse_kernel, in_specs=[whole] * 4, out_specs=[whole] * 3...  7.77 us
  transfers between devices with their start and end apart: 9, of which 6 were waited for; matrix products, arithmetic and copies ran while one was open for 3% of the time, Pallas kernels for 16%

profile of v1, /device:TPU:1, one launch (start us, length us, event | category | flops | bytes accessed | tf_op | source)
XLA Modules:
  0.0 160.1 jit_solution(15084205260829162326)
XLA Ops:
  0.6 0.0 copy-start
  0.7 0.8 copy-done
  1.5 2.1 %convolution_convert_fusion.1 = bf16[1024,32]{0,1:T(8,128)(2,1)S(1)} fusion(bf16[1024,1024]{1,0:T(8,128)(2,1)} %constant.28.clone, bf16[4,8,1024]{2,1,0:T(8,128)(2,1)S(1)} %copy-done), kind=kOutput, calls=%fused_computation.1 | convolution fusion | flops 67141632 | bytes 2228224 | tf_op jit(solution)/shard_map/strip/dot_general | solution.py:230
  3.5 0.1 copy.33
  3.6 0.1 broadcast_select_fusion.1
  3.7 0.7 collective-permute-start.1
  4.4 9.7 %collective-permute-start = (bf16[3,16,256]{2,1,0:T(8,128)(2,1)S(1)}, bf16[3,16,256]{2,1,0:T(8,128)(2,1)S(1)}, u32[]{:S(2)}, u32[]{:S(2)}) collective-permute-start(bf16[3,16,256]{2,1,0:T(8,128)(2,1)S(1)} %select_n.59), channel_id=1, source_target_pairs={{0,2},{1,15},{2,18},{3,31},{4,34},{5,47},{6,50},{7,63},{8,66},{9,7... | collective-permute-start | bytes 73736 | tf_op jit(solution)/shard_map/strip/ppermute | solution.py:240
  14.1 0.1 collective-permute-start.2
  14.2 0.6 collective-permute-start.3
  14.9 0.2 collective-permute-done
  15.1 0.0 collective-permute-done.1
  15.1 4.0 %collective-permute-done.2 = bf16[3,16,256]{2,1,0:T(8,128)(2,1)S(1)} collective-permute-done((bf16[3,16,256]{2,1,0:T(8,128)(2,1)S(1)}, bf16[3,16,256]{2,1,0:T(8,128)(2,1)S(1)}, u32[]{:S(2)}, u32[]{:S(2)}) %collective-permute-start.2) | collective-permute-done | bytes 24608 | tf_op jit(solution)/shard_map/strip/ppermute | solution.py:240
  19.1 0.0 collective-permute-done.3
  19.2 0.0 copy-start.6
  19.2 1.2 broadcast_in_dim.6
  20.4 12.1 %all-to-all-start = ((bf16[8,160,512]{2,1,0:T(8,128)(2,1)}), bf16[8,160,512]{2,1,0:T(8,128)(2,1)S(1)}, u32[]{:S(2)}, u32[]{:S(2)}) async-start(bf16[8,160,512]{2,1,0:T(8,128)(2,1)} %broadcast_in_dim.6), calls=%async_computation | async-start | bytes 2621440 | tf_op jit(solution)/shard_map/strip/all_to_all | solution.py:275
  32.5 0.0 copy-done.6
  32.5 0.2 reshape.87
  32.7 0.1 copy.28
  32.8 0.1 pad_bitcast_fusion.1
  32.9 0.1 maximum_bitcast_fusion
  33.0 0.0 copy-start.5
  33.0 0.0 copy-start.7
  33.1 0.3 copy.24
  33.4 0.4 reshape.88.forward_ref
  33.7 0.2 copy.25
  33.9 1.3 copy.26
  35.3 0.0 copy-done.5
  35.3 0.0 copy-done.7
  35.3 0.3 convolution_convert_fusion
  35.6 16.9 %all-to-all-done.parts_ref = bf16[8,160,512]{2,1,0:T(8,128)(2,1)S(1)} async-done(((bf16[8,160,512]{2,1,0:T(8,128)(2,1)}), bf16[8,160,512]{2,1,0:T(8,128)(2,1)S(1)}, u32[]{:S(2)}, u32[]{:S(2)}) %all-to-all-start) | async-done | bytes 1310752 | tf_op jit(solution)/shard_map/strip/all_to_all | solution.py:275
  52.5 23.7 %fine_forward.1 = (bf16[640,4096]{1,0:T(8,128)(2,1)S(1)}, bf16[256,4096]{1,0:T(8,128)(2,1)S(1)}, bf16[4,512,4096]{2,1,0:T(8,128)(2,1)}) custom-call(bf16[8,160,512]{2,1,0:T(8,128)(2,1)S(1)} %all-to-all-done.parts_ref, bf16[512,256]{1,0:T(8,128)(2,1)S(1)} %bitcast.41), custom_call_target="tpu_custom_call" | custom-call | tf_op jit(solution)/shard_map/fine_forward/pallas_call | solution.py:171
  76.1 0.0 copy-start.1
  76.1 2.3 %copy-done.1 = bf16[640,4096]{1,0:T(8,128)(2,1)} copy-done((bf16[640,4096]{1,0:T(8,128)(2,1)}, bf16[640,4096]{1,0:T(8,128)(2,1)S(1)}, u32[]{:S(2)}) %copy-start.1) | copy-done | bytes 5242904
  78.5 7.8 %coarse.1 = (bf16[64,4096]{1,0:T(8,128)(2,1)S(1)}, bf16[256,4096]{1,0:T(8,128)(2,1)S(1)}, bf16[32,1728]{1,0:T(8,128)(2,1)S(1)}) custom-call(bf16[256,4096]{1,0:T(8,128)(2,1)S(1)} %get-tuple-element.9.pooled_ref, bf16[576,256]{1,0:T(8,128)(2,1)S(1)} %reshape.88.forward_ref, bf16[256,576]{1,0:T(8,128)(2,1)S(1)} %bitcast.40, bf16[64,4096]{1,0:T(8,128)(2,1)S(1)} %bitcast.39), custom_call_target="tpu_custom_call" | custom-call | tf_op jit(solution)/shard_map/coarse/pallas_call | solution.py:195
  86.2 0.0 copy-start.3
  86.2 1.3 copy-done.3
  87.6 0.7 reshape.93
  88.3 4.6 %all-to-all-start.3 = ((bf16[16,2,1728]{2,1,0:T(2,128)(2,1)}), bf16[16,2,1728]{2,1,0:T(2,128)(2,1)S(1)}, u32[]{:S(2)}, u32[]{:S(2)}) async-start(bf16[16,2,1728]{2,1,0:T(2,128)(2,1)} %reshape.93), calls=%async_computation.3 | async-start | bytes 229376 | tf_op jit(solution)/shard_map/sum_two/all_to_all | solution.py:286
  92.9 0.0 copy-start.2
  92.9 2.5 %copy-done.2 = bf16[640,4096]{1,0:T(8,128)(2,1)S(1)} copy-done((bf16[640,4096]{1,0:T(8,128)(2,1)S(1)}, bf16[640,4096]{1,0:T(8,128)(2,1)}, u32[]{:S(2)}) %copy-start.2) | copy-done | bytes 5242904
  95.4 0.0 copy-start.4
  95.4 1.6 copy-done.4
  97.0 24.9 %fine_backward.1 = f32[64,128]{1,0:T(8,128)} custom-call(bf16[640,4096]{1,0:T(8,128)(2,1)S(1)} %copy-done.2, bf16[4,512,4096]{2,1,0:T(8,128)(2,1)} %get-tuple-element.12.slope_ref, bf16[256,4096]{1,0:T(8,128)(2,1)S(1)} %copy-done.4, bf16[8,256,128]{2,1,0:T(8,128)(2,1)S(1)} %copy-done.5), custom_call_target="tpu_custom_call" | custom-call | tf_op jit(solution)/shard_map/fine_backward/pallas_call | solution.py:211
  121.9 0.0 all-to-all-done.3
  121.9 5.8 %all-to-all-start.1 = ((f32[16,4,128]{2,1,0:T(4,128)}), f32[16,4,128]{2,1,0:T(4,128)S(1)}, u32[]{:S(2)}, u32[]{:S(2)}) async-start(f32[16,4,128]{2,1,0:T(4,128)} %bitcast.19), calls=%async_computation.1 | async-start | bytes 65536 | tf_op jit(solution)/shard_map/sum_one/all_to_all | solution.py:292
  127.7 0.1 reduce_sum.32
  127.8 5.7 %all-to-all-done.1 = f32[16,4,128]{2,1,0:T(4,128)S(1)} async-done(((f32[16,4,128]{2,1,0:T(4,128)}), f32[16,4,128]{2,1,0:T(4,128)S(1)}, u32[]{:S(2)}, u32[]{:S(2)}) %all-to-all-start.1) | async-done | bytes 32800 | tf_op jit(solution)/shard_map/sum_one/all_to_all | solution.py:292
  133.5 0.7 broadcast_in_dim.8
  134.2 3.7 %all-to-all-start.4 = ((bf16[16,2,1728]{2,1,0:T(2,128)(2,1)}), bf16[16,2,1728]{2,1,0:T(2,128)(2,1)S(1)}, u32[]{:S(2)}, u32[]{:S(2)}) async-start(bf16[16,2,1728]{2,1,0:T(2,128)(2,1)} %broadcast_in_dim.8), calls=%async_computation.4 | async-start | bytes 229376 | tf_op jit(solution)/shard_map/sum_two/all_to_all | solution.py:288
  137.9 6.0 %all-to-all-done.4 = bf16[16,2,1728]{2,1,0:T(2,128)(2,1)S(1)} async-done(((bf16[16,2,1728]{2,1,0:T(2,128)(2,1)}), bf16[16,2,1728]{2,1,0:T(2,128)(2,1)S(1)}, u32[]{:S(2)}, u32[]{:S(2)}) %all-to-all-start.4) | async-done | bytes 110624 | tf_op jit(solution)/shard_map/sum_two/all_to_all | solution.py:288
  143.9 0.7 broadcast_in_dim.7
  144.6 4.1 %all-to-all-start.2 = ((f32[128,4,128]{2,1,0:T(4,128)}), f32[128,4,128]{2,1,0:T(4,128)S(1)}, u32[]{:S(2)}, u32[]{:S(2)}) async-start(f32[128,4,128]{2,1,0:T(4,128)} %broadcast_in_dim.7), calls=%async_computation.2 | async-start | bytes 524288 | tf_op jit(solution)/shard_map/sum_one/all_to_all | solution.py:294
  148.7 1.3 copy.32
  150.1 0.7 reshape.94
  150.8 8.7 %all-to-all-done.2 = f32[128,4,128]{2,1,0:T(4,128)S(1)} async-done(((f32[128,4,128]{2,1,0:T(4,128)}), f32[128,4,128]{2,1,0:T(4,128)S(1)}, u32[]{:S(2)}, u32[]{:S(2)}) %all-to-all-start.2) | async-done | bytes 262176 | tf_op jit(solution)/shard_map/sum_one/all_to_all | solution.py:294
  159.5 0.6 bitcast_reduce_fusion
  (9 shorter events, 0.2 us)
Async XLA Ops:
  0.6 0.8 copy-start
  3.7 11.4 %collective-permute-start.1 = (bf16[7,16,256]{2,1,0:T(8,128)(2,1)S(1)}, bf16[7,16,256]{2,1,0:T(8,128)(2,1)S(1)}, u32[]{:S(2)}, u32[]{:S(2)}) collective-permute-start(bf16[7,16,256]{2,1,0:T(8,128)(2,1)S(1)} %select_n.62), channel_id=1, source_target_pairs={{0,0},{1,1},{2,16},{3,17},{4,32},{5,33},{6,48},{7,49},{8,64},{9,65... | collective-permute-start | bytes 172040 | tf_op jit(solution)/shard_map/strip/ppermute | solution.py:240
  4.4 10.7 %collective-permute-start = (bf16[3,16,256]{2,1,0:T(8,128)(2,1)S(1)}, bf16[3,16,256]{2,1,0:T(8,128)(2,1)S(1)}, u32[]{:S(2)}, u32[]{:S(2)}) collective-permute-start(bf16[3,16,256]{2,1,0:T(8,128)(2,1)S(1)} %select_n.59), channel_id=1, source_target_pairs={{0,2},{1,15},{2,18},{3,31},{4,34},{5,47},{6,50},{7,63},{8,66},{9,7... | collective-permute-start | bytes 73736 | tf_op jit(solution)/shard_map/strip/ppermute | solution.py:240
  14.1 5.0 %collective-permute-start.2 = (bf16[3,16,256]{2,1,0:T(8,128)(2,1)S(1)}, bf16[3,16,256]{2,1,0:T(8,128)(2,1)S(1)}, u32[]{:S(2)}, u32[]{:S(2)}) collective-permute-start(bf16[3,16,256]{2,1,0:T(8,128)(2,1)S(1)} %select_n.64), channel_id=1, source_target_pairs={{0,15},{1,2},{2,31},{3,18},{4,47},{5,34},{6,63},{7,50},{8,79},{9,6... | collective-permute-start | bytes 73736 | tf_op jit(solution)/shard_map/strip/ppermute | solution.py:240
  14.2 4.9 %collective-permute-start.3 = (bf16[7,16,256]{2,1,0:T(8,128)(2,1)S(1)}, bf16[7,16,256]{2,1,0:T(8,128)(2,1)S(1)}, u32[]{:S(2)}, u32[]{:S(2)}) collective-permute-start(bf16[7,16,256]{2,1,0:T(8,128)(2,1)S(1)} %select_n.66), channel_id=1, source_target_pairs={{0,1},{1,0},{2,17},{3,16},{4,33},{5,32},{6,49},{7,48},{8,65},{9,64... | collective-permute-start | bytes 172040 | tf_op jit(solution)/shard_map/strip/ppermute | solution.py:240
  19.2 13.3 %copy-start.6 = (bf16[32,1728]{1,0:T(8,128)(2,1)S(1)}, bf16[32,1728]{1,0:T(8,128)(2,1)}, u32[]{:S(2)}) copy-start(bf16[32,1728]{1,0:T(8,128)(2,1)} %param.8) | copy-start | bytes 331780
  20.4 32.1 %all-to-all-start = ((bf16[8,160,512]{2,1,0:T(8,128)(2,1)}), bf16[8,160,512]{2,1,0:T(8,128)(2,1)S(1)}, u32[]{:S(2)}, u32[]{:S(2)}) async-start(bf16[8,160,512]{2,1,0:T(8,128)(2,1)} %broadcast_in_dim.6), calls=%async_computation | async-start | bytes 2621440 | tf_op jit(solution)/shard_map/strip/all_to_all | solution.py:275
  33.0 2.3 %copy-start.5 = (bf16[8,256,128]{2,1,0:T(8,128)(2,1)S(1)}, bf16[8,256,128]{2,1,0:T(8,128)(2,1)}, u32[]{:S(2)}) copy-start(bf16[8,256,128]{2,1,0:T(8,128)(2,1)} %constant.27.clone.taps_ref) | copy-start | bytes 1572868
  33.0 2.3 %copy-start.7 = (bf16[64,108]{1,0:T(8,128)(2,1)S(1)}, bf16[64,108]{1,0:T(8,128)(2,1)}, u32[]{:S(2)}) copy-start(bf16[64,108]{1,0:T(8,128)(2,1)} %param.7) | copy-start | bytes 41476
  76.1 2.3 %copy-start.1 = (bf16[640,4096]{1,0:T(8,128)(2,1)}, bf16[640,4096]{1,0:T(8,128)(2,1)S(1)}, u32[]{:S(2)}) copy-start(bf16[640,4096]{1,0:T(8,128)(2,1)S(1)} %get-tuple-element.11.windows_ref) | copy-start | bytes 15728644
  86.2 1.3 copy-start.3
  88.3 33.6 %all-to-all-start.3 = ((bf16[16,2,1728]{2,1,0:T(2,128)(2,1)}), bf16[16,2,1728]{2,1,0:T(2,128)(2,1)S(1)}, u32[]{:S(2)}, u32[]{:S(2)}) async-start(bf16[16,2,1728]{2,1,0:T(2,128)(2,1)} %reshape.93), calls=%async_computation.3 | async-start | bytes 229376 | tf_op jit(solution)/shard_map/sum_two/all_to_all | solution.py:286
  92.9 2.5 %copy-start.2 = (bf16[640,4096]{1,0:T(8,128)(2,1)S(1)}, bf16[640,4096]{1,0:T(8,128)(2,1)}, u32[]{:S(2)}) copy-start(bf16[640,4096]{1,0:T(8,128)(2,1)} %copy-done.1) | copy-start | bytes 15728644
  95.4 1.6 copy-start.4
  121.9 11.6 %all-to-all-start.1 = ((f32[16,4,128]{2,1,0:T(4,128)}), f32[16,4,128]{2,1,0:T(4,128)S(1)}, u32[]{:S(2)}, u32[]{:S(2)}) async-start(f32[16,4,128]{2,1,0:T(4,128)} %bitcast.19), calls=%async_computation.1 | async-start | bytes 65536 | tf_op jit(solution)/shard_map/sum_one/all_to_all | solution.py:292
  134.2 9.7 %all-to-all-start.4 = ((bf16[16,2,1728]{2,1,0:T(2,128)(2,1)}), bf16[16,2,1728]{2,1,0:T(2,128)(2,1)S(1)}, u32[]{:S(2)}, u32[]{:S(2)}) async-start(bf16[16,2,1728]{2,1,0:T(2,128)(2,1)} %broadcast_in_dim.8), calls=%async_computation.4 | async-start | bytes 229376 | tf_op jit(solution)/shard_map/sum_two/all_to_all | solution.py:288
  144.6 14.9 %all-to-all-start.2 = ((f32[128,4,128]{2,1,0:T(4,128)}), f32[128,4,128]{2,1,0:T(4,128)S(1)}, u32[]{:S(2)}, u32[]{:S(2)}) async-start(f32[128,4,128]{2,1,0:T(4,128)} %broadcast_in_dim.7), calls=%async_computation.2 | async-start | bytes 524288 | tf_op jit(solution)/shard_map/sum_one/all_to_all | solution.py:294

commit v2 on v1

v2 whole, which is shorter than its diff:
```python
import jax
import jax.numpy as jnp
import numpy as np
from jax import lax
from jax.experimental import pallas as pl
from jax.experimental.pallas import tpu as pltpu
from jax.sharding import Mesh, PartitionSpec as P

C0 = 4
C1 = 64
Z = 64
HZ = 32
CELLS = 4096
ROWS = 4
TILE = 512
WIDE = 2048
CHIP = ("x", "zh", "zl", "y", "core")
F32 = jnp.float32
BF16 = jnp.bfloat16


def split_depth():
    sort = np.zeros((1024, 1024), np.float32)
    for y in range(16):
        for z in range(Z):
            sort[y * Z + z, ((y % 2) * 2 + z % 2) * 256 + (y // 2) * HZ + z // 2] = 1
    return sort


def window_taps():
    place = {(1, 1): 0, (0, 0): 1, (0, 1): 2, (1, 0): 3}
    taps = np.zeros((8, 256, 128), np.float32)
    for cell in range(8):
        a, b, c = cell // 4, cell // 2 % 2, cell % 2
        for x in range(4):
            for y_key, y in place.items():
                for z_key, z in place.items():
                    dx, dy, dz = x - a, y - b, z - c
                    if min(dx, dy, dz) < 0 or max(dx, dy, dz) > 2:
                        continue
                    row = x * 64 + y_key[0] * 32 + z_key[0] * 16 + y_key[1] * 8 + z_key[1] * 4
                    for i in range(C0):
                        taps[cell, row + i, (9 * dx + 3 * dy + dz) * C0 + i] = 1
    return taps


def depth_of(shape):
    return lax.broadcasted_iota(jnp.int32, shape, 1) % HZ


def move(values, step):
    return pltpu.roll(values, step % values.shape[1], 1)


def from_below(values, depth):
    return jnp.where(depth != 0, move(values, 1), 0.0)


def from_above(values, depth):
    return jnp.where(depth != HZ - 1, move(values, -1), 0.0)


def place_windows(cells, windows_ref, at):
    depth = depth_of((8, CELLS))
    low = lax.broadcasted_iota(jnp.int32, (8, CELLS), 0) < 4
    cells = cells.astype(F32)
    even, odd = cells[:8], cells[8:]
    for shifted, (top, bottom) in enumerate(((even, odd), (move(even, -HZ), move(odd, HZ)))):
        here = pl.multiple_of(at + 32 * shifted, 32)
        windows_ref[pl.ds(here, 16), :] = jnp.concatenate([top, bottom], axis=0).astype(BF16)
        moved = [
            jnp.where(low, from_above(half, depth), from_below(half, depth))
            for half in (top, bottom)
        ]
        windows_ref[pl.ds(here + 16, 16), :] = jnp.concatenate(moved, axis=0).astype(BF16)


def levels_kernel(
    side_ref, own_ref, other_ref, fine_ref, forward_ref, backward_ref, cot_ref, taps_ref,
    feature_ref, grad_ref,
    windows_ref, slope_ref, pooled_ref, wide_ref, moved_ref, back_ref, sum_ref,
):
    side = side_ref[0]

    def row_of(ref, j):
        return jnp.concatenate([ref[c, 16 * j : 16 * j + 16, :] for c in range(8)], axis=1)

    for j in range(4):
        place_windows(row_of(own_ref, j), windows_ref, 64 * (3 + j))
    for j in range(3):
        place_windows(row_of(own_ref, 4 + j), windows_ref, 64 * (j + 7 * side))
        place_windows(row_of(other_ref, j), windows_ref, 64 * (j + 7 * (1 - side)))

    def fine_step(step, _):
        row, tile = step // (CELLS // WIDE), step % (CELLS // WIDE)
        lanes = pl.ds(pl.multiple_of(tile * WIDE, WIDE), WIDE)
        window = windows_ref[pl.ds(pl.multiple_of(row * 128, 128), 256), lanes]
        pre = jnp.dot(fine_ref[...], window, preferred_element_type=F32)
        total = None
        for cell in range(8):
            value = pre[C1 * cell : C1 * cell + C1].astype(BF16)
            bent = jnp.tanh(value)
            gate = bent + 0.65 / 0.35
            act = value * gate
            slope_ref[row * 8 + cell, :, lanes] = gate + value * (1.0 - bent * bent)
            total = act if total is None else total + act
        pooled_ref[pl.ds(pl.multiple_of(row * C1, C1), C1), lanes] = (
            total.astype(F32) * (0.125 * 0.35)
        ).astype(BF16)
        return 0

    lax.fori_loop(0, ROWS * CELLS // WIDE, fine_step, 0)

    for tile in range(CELLS // TILE):
        lanes = slice(tile * TILE, tile * TILE + TILE)
        wide_ref[:, lanes] = jnp.dot(forward_ref[...], pooled_ref[:, lanes], preferred_element_type=F32)
    depth = depth_of((16, CELLS))
    for block in range(4):
        def term(dy, dz):
            at = 64 * (3 * dy + dz) + 16 * block
            return wide_ref[at : at + 16, :]

        def column(dz):
            return term(1, dz) + move(term(0, dz), HZ) + move(term(2, dz), -HZ)

        pre = column(1) + from_below(column(0), depth) + from_above(column(2), depth)
        rows = slice(16 * block, 16 * block + 16)
        bent = jnp.tanh(pre)
        gate = 0.65 + 0.35 * bent
        feature_ref[rows, :] = (pre * gate).astype(BF16)
        slope = gate + 0.35 * pre * (1.0 - bent * bent)
        grads = (cot_ref[rows, :].astype(F32) * slope).astype(BF16).astype(F32)
        for dy in range(3):
            here = grads if dy == 1 else move(grads, HZ * (dy - 1))
            for dz in range(3):
                there = here if dz == 1 else (from_above if dz == 0 else from_below)(here, depth)
                at = 64 * (3 * dy + dz) + 16 * block
                moved_ref[at : at + 16, :] = there.astype(BF16)
    for tile in range(CELLS // TILE):
        lanes = slice(tile * TILE, tile * TILE + TILE)
        back_ref[:, lanes] = jnp.dot(
            backward_ref[...], moved_ref[:, lanes], preferred_element_type=F32
        ).astype(BF16)
    grad = lax.dot_general(
        moved_ref[...], pooled_ref[...], (((1,), (1,)), ((), ())), preferred_element_type=F32
    )
    for tap in range(9):
        both = grad[64 * tap : 64 * tap + 32, :192] + grad[64 * tap + 32 : 64 * tap + 64, 64:]
        for dx in range(3):
            at = dx * 576 + tap * 64
            grad_ref[:, at : at + 64] = both[:, 64 * dx : 64 * dx + 64]
    grad_ref[:, 1728:1792] = jnp.zeros((32, 64), F32)

    sum_ref[...] = jnp.zeros_like(sum_ref)

    def back_step(row, _):
        window = windows_ref[pl.ds(pl.multiple_of(row * 128, 128), 256), :]
        back = back_ref[pl.ds(pl.multiple_of(row * C1, C1), C1), :]
        grads = jnp.concatenate([slope_ref[row * 8 + cell] * back for cell in range(8)], axis=0)
        sum_ref[...] += lax.dot_general(
            grads, window, (((1,), (1,)), ((), ())), preferred_element_type=F32
        )
        return 0

    lax.fori_loop(0, ROWS, back_step, 0)
    total = jnp.zeros((C1, 128), F32)
    for cell in range(8):
        whole = sum_ref[C1 * cell : C1 * cell + C1, :]
        high = whole.astype(BF16)
        low = (whole - high.astype(F32)).astype(BF16)
        total += jnp.dot(high, taps_ref[cell], preferred_element_type=F32)
        total += jnp.dot(low, taps_ref[cell], preferred_element_type=F32)
    total = total * (0.125 * 0.35)
    for half in range(2):
        for part in range(2):
            at = 32 * half + 16 * part
            grad_ref[16 * half : 16 * half + 16, 1792 + 128 * part : 1920 + 128 * part] = total[at : at + 16]


def levels(side, own, other, fine, forward, backward, cot, taps):
    whole = pl.BlockSpec(memory_space=pltpu.VMEM)
    return pl.pallas_call(
        levels_kernel,
        in_specs=[pl.BlockSpec(memory_space=pltpu.SMEM)] + [whole] * 7,
        out_specs=[whole] * 2,
        out_shape=[
            jax.ShapeDtypeStruct((64, CELLS), BF16),
            jax.ShapeDtypeStruct((32, 2048), F32),
        ],
        scratch_shapes=[
            pltpu.VMEM((640, CELLS), BF16),
            pltpu.VMEM((32, C1, CELLS), BF16),
            pltpu.VMEM((ROWS * C1, CELLS), BF16),
            pltpu.VMEM((576, CELLS), F32),
            pltpu.VMEM((576, CELLS), BF16),
            pltpu.VMEM((ROWS * C1, CELLS), BF16),
            pltpu.VMEM((512, 256), F32),
        ],
        compiler_params=pltpu.CompilerParams(vmem_limit_bytes=58 << 20),
        name="levels",
    )(side, own, other, fine, forward, backward, cot, taps)


def swap(values):
    return lax.ppermute(values, "core", [(0, 1), (1, 0)])


def by_core(side, mine, other, dim):
    return jnp.where(
        side == 0, jnp.concatenate([mine, other], dim), jnp.concatenate([other, mine], dim)
    )


def pair_list(target):
    pairs = []
    for gx in range(8):
        for chip in range(8):
            for core in range(2):
                to_x, to_chip, to_core = target(gx, chip, core)
                pairs.append(((gx * 8 + chip) * 2 + core, (to_x * 8 + to_chip % 8) * 2 + to_core))
    return pairs


def strip_parts(density, side):
    sort = jnp.asarray(split_depth(), BF16)
    sorted_cells = jnp.dot(density.reshape(32, 1024), sort, preferred_element_type=F32).astype(BF16)
    block = sorted_cells.reshape(C0, 8, 4, 256).transpose(1, 2, 0, 3).reshape(8, 16, 256)
    kept = jnp.where(side == 0, block[:4], block[4:])
    half = by_core(side, kept, swap(jnp.where(side == 0, block[4:], block[:4])), 2)
    main = lax.ppermute(half, CHIP, pair_list(lambda gx, chip, core: (chip, gx, core)))
    rim = lax.ppermute(
        jnp.where(side == 0, half[:3], half[1:]),
        CHIP,
        pair_list(lambda gx, chip, core: (chip, gx + 2 * core - 1, 1 - core)),
    )
    part = jnp.concatenate([main, rim], 0).reshape(112, 512)
    own = lax.all_to_all(jnp.broadcast_to(part[None], (8, 112, 512)), ("x", "zh"), 0, 0)
    other = swap(jnp.where(side == 0, own[:, 16:64], own[:, :48]))
    return own, other


def coarse_weights(weight_two):
    taps = weight_two.reshape(32, 3, 9, C1)
    both = jnp.stack([jnp.pad(taps, ((0, 0), (r, 1 - r), (0, 0), (0, 0))) for r in range(2)])
    forward = both.transpose(3, 0, 1, 2, 4).reshape(576, 256)
    return forward, forward.T


def sum_grads(terms, side):
    mine = jnp.where(side == 0, terms[:16], terms[16:])
    mine = mine + swap(jnp.where(side == 0, terms[16:], terms[:16]))
    copies = jnp.broadcast_to(mine.astype(BF16)[None], (8, 16, 2048))
    summed = lax.all_to_all(copies, ("zl", "y"), 0, 0).astype(F32).sum(0)
    copies = jnp.broadcast_to(summed[None, :, 1792:], (8, 16, 256))
    one = lax.all_to_all(copies, ("x", "zh"), 0, 0).sum(0)
    grad_two = by_core(side, summed[:, :1728], swap(summed[:, :1728]), 0)
    one = by_core(side, one, swap(one), 0)
    grad_one = one.reshape(2, 16, 2, 128).transpose(0, 2, 1, 3).reshape(C1, 128)[:, :108]
    return grad_one, grad_two


def body(density, weight_one, weight_two, feature_cot):
    taps = jnp.asarray(window_taps(), BF16)
    side = lax.axis_index("core")
    with jax.named_scope("strip"):
        own, other = strip_parts(density, side)
    with jax.named_scope("weights"):
        fine_weight = jnp.einsum(
            "ok,srk->sor", jnp.pad(weight_one, ((0, 0), (0, 20))), taps, preferred_element_type=F32
        ).astype(BF16).reshape(512, 256)
        forward, backward = coarse_weights(weight_two)
        cot = feature_cot.transpose(1, 0, 2).reshape(64, CELLS)
    features, terms = levels(
        side.astype(jnp.int32).reshape(1), own, other, fine_weight, forward, backward, cot, taps
    )
    features = features.reshape(2, 32, CELLS).transpose(1, 0, 2)
    with jax.named_scope("sums"):
        grad_one, grad_two = sum_grads(terms, side)
    return features, grad_one, grad_two


def solution(mesh):
    fine_mesh = Mesh(mesh.devices.reshape(4, 2, 2, 4, 2), CHIP)
    gx, gy = ("x", "zh"), ("zl", "y", "core")
    return jax.shard_map(
        body,
        mesh=fine_mesh,
        in_specs=(P(None, gx, gy), P(), P(gx, None), P(gx, gy, None)),
        out_specs=(P(gx, gy, None), P(), P(gx, None)),
        check_vma=False,
    )
```

time: 161 us -> 110 us (0.68)
  Pallas kernels: 56.3 us -> 26.8 us
  waiting for transfers between devices: 41.5 us -> 20.2 us
  blocking collectives: 0 us -> 16.7 us
  starting transfers between devices: 41.4 us -> 30.9 us
  local copies, waits for them, and re-layouts: 16.7 us -> 7.9 us
  other arithmetic: 1.04 us -> 3.21 us
    pallas_call x3 -> x1, Pallas kernels: 56.3 us -> 26.8 us  [levels(): pl.pallas_call(levels_kernel, in_specs=[pl.BlockSpec(memory_space=pltpu.S...]
    all_to_all x5 -> x2, waiting for transfers between devices: 37.2 us -> 16.8 us  [the longest x1 12.5 us: strip_parts(): lax.all_to_all(jnp.broadcast_to(part[None], (8, 112, 512)), ('x', 'zh'),...]
    all_to_all x0 -> x1, blocking collectives: none -> 16.7 us  [sum_grads(): summed = lax.all_to_all(copies, ('zl', 'y'), 0, 0).astype(F32).sum(0)]
    all_to_all x5 -> x2, starting transfers between devices: 30.3 us -> 18.1 us  [the longest x1 14 us: strip_parts(): lax.all_to_all(jnp.broadcast_to(part[None], (8, 112, 512)), ('x', 'zh'),...]
    unnamed x17, local copies, waits for them, and re-layouts: 8.63 us -> 1.15 us
    select_n x3 -> x7, other arithmetic: 0.12 us -> 1.93 us  [the longest x1 1.04 us: sum_grads(): mine = mine + swap(jnp.where(side == 0, terms[16:], terms[:16]))]
    ppermute x4 -> x7, starting transfers between devices: 11.1 us -> 12.8 us  [the longest x1 6.69 us: strip_parts(): lax.ppermute(jnp.where(side == 0, half[:3], half[1:]), CHIP, pair_list(la...]
    ppermute x4 -> x7, waiting for transfers between devices: 4.25 us -> 3.4 us  [the longest x5 2.07 us: swap(): return lax.ppermute(values, 'core', [(0, 1), (1, 0)])]
  transfers between devices with their start and end apart: 9 -> 9, of which waited for: 6 -> 6; matrix products, arithmetic and copies ran while one was open for 3% -> 6% of each run, Pallas kernels for 16% -> 0%
where the time goes in v2:
time: 110 us; the launch traced here: 109 us
  starting transfers between devices  30.9 us (28%)
  Pallas kernels  26.8 us (24%)
  waiting for transfers between devices  20.2 us (18%)
  blocking collectives  16.7 us (15%)
  local copies, waits for them, and re-layouts  7.9 us (7%)
  other arithmetic  3.21 us (3%)
  matrix products  3.06 us (3%)
    pallas_call x1, Pallas kernels, levels(): pl.pallas_call(levels_kernel, in_specs=[pl.BlockSpec(memory_space=pltpu.S...  26.8 us
    all_to_all x1, blocking collectives, sum_grads(): summed = lax.all_to_all(copies, ('zl', 'y'), 0, 0).astype(F32).sum(0)  16.7 us
    all_to_all x1, starting transfers between devices, strip_parts(): lax.all_to_all(jnp.broadcast_to(part[None], (8, 112, 512)), ('x', 'zh'),...  14 us
    all_to_all x1, waiting for transfers between devices, strip_parts(): lax.all_to_all(jnp.broadcast_to(part[None], (8, 112, 512)), ('x', 'zh'),...  12.5 us
    ppermute x1, starting transfers between devices, strip_parts(): lax.ppermute(jnp.where(side == 0, half[:3], half[1:]), CHIP, pair_list(la...  6.69 us
    ppermute x5, starting transfers between devices, swap(): return lax.ppermute(values, 'core', [(0, 1), (1, 0)])  5.42 us
    all_to_all x1, waiting for transfers between devices, sum_grads(): one = lax.all_to_all(copies, ('x', 'zh'), 0, 0).sum(0)  4.25 us
    all_to_all x1, starting transfers between devices, sum_grads(): one = lax.all_to_all(copies, ('x', 'zh'), 0, 0).sum(0)  4.08 us
  transfers between devices with their start and end apart: 9, of which 6 were waited for; matrix products, arithmetic and copies ran while one was open for 6% of the time, Pallas kernels for 0%

profile of v2, /device:TPU:1, one launch (start us, length us, event | category | flops | bytes accessed | tf_op | source)
XLA Modules:
  0.0 109.5 jit_solution(16838420415930551445)
XLA Ops:
  0.6 0.0 copy-start
  0.6 0.8 copy-done
  1.5 2.1 %convolution_convert_fusion.1 = bf16[1024,32]{0,1:T(8,128)(2,1)S(1)} fusion(bf16[1024,1024]{1,0:T(8,128)(2,1)} %constant.15.clone, bf16[4,8,1024]{2,1,0:T(8,128)(2,1)S(1)} %copy-done), kind=kOutput, calls=%fused_computation.1 | convolution fusion | flops 67141632 | bytes 2228224 | tf_op jit(solution)/shard_map/strip/dot_general | solution.py:226
  3.5 0.0 copy-start.6
  3.6 1.5 %collective-permute-start = (bf16[4,16,256]{2,0,1:T(4,128)(2,1)S(1)}, bf16[4,16,256]{2,0,1:T(4,128)(2,1)S(1)}, u32[]{:S(2)}, u32[]{:S(2)}) collective-permute-start(bf16[4,16,256]{2,0,1:T(4,128)(2,1)S(1)} %bitcast.49), channel_id=1, source_target_pairs={{0,1},{1,0},{2,3},{3,2},{4,5},{5,4},{6,7},{7,6},{8,9},{9,8},{10,11... | collective-permute-start | bytes 98312 | tf_op jit(solution)/shard_map/strip/ppermute | solution.py:205
  5.1 0.9 collective-permute-done
  6.0 0.7 collective-permute-start.1
  6.7 0.1 slice_select_fusion.2
  6.8 6.7 %collective-permute-start.2 = (bf16[3,16,512]{2,0,1:T(4,128)(2,1)S(1)}, bf16[3,16,512]{2,0,1:T(4,128)(2,1)S(1)}, u32[]{:S(2)}, u32[]{:S(2)}) collective-permute-start(bf16[3,16,512]{2,0,1:T(4,128)(2,1)S(1)} %slice_select_fusion.2), channel_id=1, source_target_pairs={{0,15},{1,2},{2,31},{3,18},{4,47},{5,34},{6,63},{7,50},{8,79},{9,6... | collective-permute-start | bytes 147464 | tf_op jit(solution)/shard_map/strip/ppermute | solution.py:231
  13.4 1.3 %collective-permute-done.2 = bf16[3,16,512]{2,0,1:T(4,128)(2,1)S(1)} collective-permute-done((bf16[3,16,512]{2,0,1:T(4,128)(2,1)S(1)}, bf16[3,16,512]{2,0,1:T(4,128)(2,1)S(1)}, u32[]{:S(2)}, u32[]{:S(2)}) %collective-permute-start.2) | collective-permute-done | bytes 49184 | tf_op jit(solution)/shard_map/strip/ppermute | solution.py:231
  14.8 0.0 collective-permute-done.1
  14.8 0.1 pad_maximum_fusion
  14.9 1.0 broadcast_in_dim.9
  15.9 14.0 %all-to-all-start = ((bf16[8,112,512]{2,1,0:T(8,128)(2,1)}), bf16[8,112,512]{2,1,0:T(8,128)(2,1)S(1)}, u32[]{:S(2)}, u32[]{:S(2)}) async-start(bf16[8,112,512]{2,1,0:T(8,128)(2,1)} %broadcast_in_dim.9), calls=%async_computation | async-start | bytes 1835008 | tf_op jit(solution)/shard_map/strip/all_to_all | solution.py:237
  29.9 0.0 copy-done.6
  29.9 0.2 reshape.53
  30.2 0.1 copy.39
  30.2 12.5 %all-to-all-done.own_ref = bf16[8,112,512]{2,1,0:T(8,128)(2,1)S(1)} async-done(((bf16[8,112,512]{2,1,0:T(8,128)(2,1)}), bf16[8,112,512]{2,1,0:T(8,128)(2,1)S(1)}, u32[]{:S(2)}, u32[]{:S(2)}) %all-to-all-start) | async-done | bytes 917536 | tf_op jit(solution)/shard_map/strip/all_to_all | solution.py:237
  42.8 0.0 copy-start.1
  42.8 0.1 collective-permute-start.3
  42.9 0.1 pad_bitcast_fusion.1
  43.0 0.0 copy-start.4
  43.0 0.1 maximum_bitcast_fusion
  43.1 0.0 copy-start.3
  43.1 0.0 copy-start.7
  43.2 0.3 copy.34
  43.5 0.2 copy-done.1
  43.7 0.4 reshape.54.forward_ref
  44.1 0.0 copy-start.2
  44.1 0.9 copy.35
  45.0 0.0 copy-done.4
  45.0 1.1 copy.36
  46.1 0.0 copy-done.3
  46.1 0.0 copy-done.7
  46.1 1.0 convolution_convert_fusion
  47.1 0.0 collective-permute-done.3.other_ref
  47.1 0.0 copy-done.2
  47.1 26.8 %levels.1 = (bf16[64,4096]{1,0:T(8,128)(2,1)}, f32[32,2048]{1,0:T(8,128)}) custom-call(s32[1]{0:T(128)} %bitcast.side_ref, bf16[8,112,512]{2,1,0:T(8,128)(2,1)} %copy-done.1, bf16[8,48,512]{2,1,0:T(8,128)(2,1)} %collective-permute-done.3.other_ref, bf16[512,256]{1,0:T(8,128)(2,1)} %bitcast.39, bf16[576,256]{1,0:T(8,128)(2,1)} %copy-done.2, ...), custom_call_target="tpu_custom_call" | custom-call | tf_op jit(solution)/shard_map/levels/pallas_call | solution.py:182
  73.9 0.0 copy-start.5
  73.9 1.0 slice_select_fusion.1
  74.9 0.4 collective-permute-start.4
  75.3 1.1 collective-permute-done.4
  76.4 1.0 add_convert_fusion
  77.4 16.7 %all_to_all.15 = bf16[8,16,2048]{2,1,0:T(8,128)(2,1)S(1)} all-to-all(bf16[8,16,2048]{2,1,0:T(8,128)(2,1)S(1)} %broadcast_in_dim.10), channel_id=1, replica_groups=mesh['x'=4,'zh'=2,'zl'=2,'y'=4,'core'=2] {'zl','y'}, dimensions={0} | all-to-all | bytes 1048576 | tf_op jit(solution)/shard_map/sums/all_to_all | solution.py:253
  94.1 0.1 convert_reduce_fusion
  94.1 0.7 broadcast_in_dim.22
  94.8 4.1 %all-to-all-start.2 = ((f32[8,16,256]{2,1,0:T(8,128)}), f32[8,16,256]{2,1,0:T(8,128)S(1)}, u32[]{:S(2)}, u32[]{:S(2)}) async-start(f32[8,16,256]{2,1,0:T(8,128)} %broadcast_in_dim.22), calls=%async_computation.2 | async-start | bytes 262144 | tf_op jit(solution)/shard_map/sums/all_to_all | solution.py:255
  98.9 1.2 %collective-permute-start.6 = (f32[16,1728]{1,0:T(8,128)S(1)}, f32[16,1728]{1,0:T(8,128)S(1)}, u32[]{:S(2)}, u32[]{:S(2)}) collective-permute-start(f32[16,1728]{1,0:T(8,128)S(1)} %slice.59), channel_id=1, source_target_pairs={{0,1},{1,0},{2,3},{3,2},{4,5},{5,4},{6,7},{7,6},{8,9},{9,8},{10,11... | collective-permute-start | bytes 331784 | tf_op jit(solution)/shard_map/sums/ppermute | solution.py:205
  100.1 0.0 copy-done.5
  100.1 1.3 %copy.43 = bf16[2,32,4096]{2,0,1:T(2,128)(2,1)} copy(bf16[2,32,4096]{2,1,0:T(8,128)(2,1)S(1)} %bitcast.41) | data formatting | bytes 1048576 | tf_op jit(solution)/shard_map/reshape | solution.py:276
  101.4 4.2 %all-to-all-done.2 = f32[8,16,256]{2,1,0:T(8,128)S(1)} async-done(((f32[8,16,256]{2,1,0:T(8,128)}), f32[8,16,256]{2,1,0:T(8,128)S(1)}, u32[]{:S(2)}, u32[]{:S(2)}) %all-to-all-start.2) | async-done | bytes 131104 | tf_op jit(solution)/shard_map/sums/all_to_all | solution.py:255
  105.7 2.3 %collective-permute-start.5 = (f32[16,256]{1,0:T(8,128)S(1)}, f32[16,256]{1,0:T(8,128)S(1)}, u32[]{:S(2)}, u32[]{:S(2)}) collective-permute-start(f32[16,256]{1,0:T(8,128)S(1)} %reduce_sum.19), channel_id=1, source_target_pairs={{0,1},{1,0},{2,3},{3,2},{4,5},{5,4},{6,7},{7,6},{8,9},{9,8},{10,11... | collective-permute-start | bytes 49160 | tf_op jit(solution)/shard_map/sums/ppermute | solution.py:205
  108.0 0.0 collective-permute-done.6
  108.0 0.7 maximum_select_fusion
  108.7 0.1 collective-permute-done.5
  108.9 0.6 copy.38
  (11 shorter events, 0.3 us)
Async XLA Ops:
  0.6 0.8 copy-start
  3.5 26.4 %copy-start.6 = (bf16[32,1728]{1,0:T(8,128)(2,1)S(1)}, bf16[32,1728]{1,0:T(8,128)(2,1)}, u32[]{:S(2)}) copy-start(bf16[32,1728]{1,0:T(8,128)(2,1)} %param.8) | copy-start | bytes 331780
  3.6 2.4 %collective-permute-start = (bf16[4,16,256]{2,0,1:T(4,128)(2,1)S(1)}, bf16[4,16,256]{2,0,1:T(4,128)(2,1)S(1)}, u32[]{:S(2)}, u32[]{:S(2)}) collective-permute-start(bf16[4,16,256]{2,0,1:T(4,128)(2,1)S(1)} %bitcast.49), channel_id=1, source_target_pairs={{0,1},{1,0},{2,3},{3,2},{4,5},{5,4},{6,7},{7,6},{8,9},{9,8},{10,11... | collective-permute-start | bytes 98312 | tf_op jit(solution)/shard_map/strip/ppermute | solution.py:205
  6.0 8.8 %collective-permute-start.1 = (bf16[4,16,512]{2,0,1:T(4,128)(2,1)S(1)}, bf16[4,16,512]{2,0,1:T(4,128)(2,1)S(1)}, u32[]{:S(2)}, u32[]{:S(2)}) collective-permute-start(bf16[4,16,512]{2,0,1:T(4,128)(2,1)S(1)} %maximum_select_fusion.1), channel_id=1, source_target_pairs={{0,0},{1,1},{2,16},{3,17},{4,32},{5,33},{6,48},{7,49},{8,64},{9,65... | collective-permute-start | bytes 196616 | tf_op jit(solution)/shard_map/strip/ppermute | solution.py:230
  6.8 8.0 %collective-permute-start.2 = (bf16[3,16,512]{2,0,1:T(4,128)(2,1)S(1)}, bf16[3,16,512]{2,0,1:T(4,128)(2,1)S(1)}, u32[]{:S(2)}, u32[]{:S(2)}) collective-permute-start(bf16[3,16,512]{2,0,1:T(4,128)(2,1)S(1)} %slice_select_fusion.2), channel_id=1, source_target_pairs={{0,15},{1,2},{2,31},{3,18},{4,47},{5,34},{6,63},{7,50},{8,79},{9,6... | collective-permute-start | bytes 147464 | tf_op jit(solution)/shard_map/strip/ppermute | solution.py:231
  15.9 26.9 %all-to-all-start = ((bf16[8,112,512]{2,1,0:T(8,128)(2,1)}), bf16[8,112,512]{2,1,0:T(8,128)(2,1)S(1)}, u32[]{:S(2)}, u32[]{:S(2)}) async-start(bf16[8,112,512]{2,1,0:T(8,128)(2,1)} %broadcast_in_dim.9), calls=%async_computation | async-start | bytes 1835008 | tf_op jit(solution)/shard_map/strip/all_to_all | solution.py:237
  42.8 0.9 copy-start.1
  42.8 4.3 %collective-permute-start.3 = (bf16[8,48,512]{2,1,0:T(8,128)(2,1)S(1)}, bf16[8,48,512]{2,1,0:T(8,128)(2,1)}, u32[]{:S(2)}, u32[]{:S(2)}) collective-permute-start(bf16[8,48,512]{2,1,0:T(8,128)(2,1)S(1)} %slice_select_fusion), channel_id=1, source_target_pairs={{0,1},{1,0},{2,3},{3,2},{4,5},{5,4},{6,7},{7,6},{8,9},{9,8},{10,11... | collective-permute-start | bytes 1179656 | tf_op jit(solution)/shard_map/strip/ppermute | solution.py:205
  43.0 2.0 %copy-start.4 = (bf16[32,2,4096]{2,1,0:T(2,128)(2,1)S(1)}, bf16[32,2,4096]{2,1,0:T(2,128)(2,1)}, u32[]{:S(2)}) copy-start(bf16[32,2,4096]{2,1,0:T(2,128)(2,1)} %param.9) | copy-start | bytes 1572868
  43.1 3.0 %copy-start.3 = (bf16[8,256,128]{2,1,0:T(8,128)(2,1)S(1)}, bf16[8,256,128]{2,1,0:T(8,128)(2,1)}, u32[]{:S(2)}) copy-start(bf16[8,256,128]{2,1,0:T(8,128)(2,1)} %constant.14.clone.taps_ref) | copy-start | bytes 1572868
  43.1 3.0 %copy-start.7 = (bf16[64,108]{1,0:T(8,128)(2,1)S(1)}, bf16[64,108]{1,0:T(8,128)(2,1)}, u32[]{:S(2)}) copy-start(bf16[64,108]{1,0:T(8,128)(2,1)} %param.7) | copy-start | bytes 41476
  44.1 3.1 %copy-start.2 = (bf16[576,256]{1,0:T(8,128)(2,1)}, bf16[576,256]{1,0:T(8,128)(2,1)S(1)}, u32[]{:S(2)}) copy-start(bf16[576,256]{1,0:T(8,128)(2,1)S(1)} %reshape.54.forward_ref) | copy-start | bytes 884740
  73.9 26.2 %copy-start.5 = (bf16[64,4096]{1,0:T(8,128)(2,1)S(1)}, bf16[64,4096]{1,0:T(8,128)(2,1)}, u32[]{:S(2)}) copy-start(bf16[64,4096]{1,0:T(8,128)(2,1)} %get-tuple-element.5) | copy-start | bytes 1572868
  74.9 1.4 %collective-permute-start.4 = (f32[16,2048]{1,0:T(8,128)S(1)}, f32[16,2048]{1,0:T(8,128)S(1)}, u32[]{:S(2)}, u32[]{:S(2)}) collective-permute-start(f32[16,2048]{1,0:T(8,128)S(1)} %slice_select_fusion.1), channel_id=1, source_target_pairs={{0,1},{1,0},{2,3},{3,2},{4,5},{5,4},{6,7},{7,6},{8,9},{9,8},{10,11... | collective-permute-start | bytes 393224 | tf_op jit(solution)/shard_map/sums/ppermute | solution.py:205
  94.8 10.8 %all-to-all-start.2 = ((f32[8,16,256]{2,1,0:T(8,128)}), f32[8,16,256]{2,1,0:T(8,128)S(1)}, u32[]{:S(2)}, u32[]{:S(2)}) async-start(f32[8,16,256]{2,1,0:T(8,128)} %broadcast_in_dim.22), calls=%async_computation.2 | async-start | bytes 262144 | tf_op jit(solution)/shard_map/sums/all_to_all | solution.py:255
  98.9 9.1 %collective-permute-start.6 = (f32[16,1728]{1,0:T(8,128)S(1)}, f32[16,1728]{1,0:T(8,128)S(1)}, u32[]{:S(2)}, u32[]{:S(2)}) collective-permute-start(f32[16,1728]{1,0:T(8,128)S(1)} %slice.59), channel_id=1, source_target_pairs={{0,1},{1,0},{2,3},{3,2},{4,5},{5,4},{6,7},{7,6},{8,9},{9,8},{10,11... | collective-permute-start | bytes 331784 | tf_op jit(solution)/shard_map/sums/ppermute | solution.py:205
  105.7 3.2 %collective-permute-start.5 = (f32[16,256]{1,0:T(8,128)S(1)}, f32[16,256]{1,0:T(8,128)S(1)}, u32[]{:S(2)}, u32[]{:S(2)}) collective-permute-start(f32[16,256]{1,0:T(8,128)S(1)} %reduce_sum.19), channel_id=1, source_target_pairs={{0,1},{1,0},{2,3},{3,2},{4,5},{5,4},{6,7},{7,6},{8,9},{9,8},{10,11... | collective-permute-start | bytes 49160 | tf_op jit(solution)/shard_map/sums/ppermute | solution.py:205

commit v3 on v2

--- a/solution.py
+++ b/solution.py
@@ -14,6 +14,7 @@
 ROWS = 4
 TILE = 512
 WIDE = 2048
+SENT = 2304
 CHIP = ("x", "zh", "zl", "y", "core")
 F32 = jnp.float32
 BF16 = jnp.bfloat16
@@ -77,24 +78,24 @@
 
 def levels_kernel(
     side_ref, own_ref, other_ref, fine_ref, forward_ref, backward_ref, cot_ref, taps_ref,
-    feature_ref, grad_ref,
+    feature_ref, keep_ref, send_ref,
     windows_ref, slope_ref, pooled_ref, wide_ref, moved_ref, back_ref, sum_ref,
 ):
     side = side_ref[0]
 
-    def row_of(ref, j):
-        return jnp.concatenate([ref[c, 16 * j : 16 * j + 16, :] for c in range(8)], axis=1)
-
-    for j in range(4):
-        place_windows(row_of(own_ref, j), windows_ref, 64 * (3 + j))
-    for j in range(3):
-        place_windows(row_of(own_ref, 4 + j), windows_ref, 64 * (j + 7 * side))
-        place_windows(row_of(other_ref, j), windows_ref, 64 * (j + 7 * (1 - side)))
-
-    def fine_step(step, _):
+    for x in range(10):
+        rows = pl.ds(pl.multiple_of(16 * (x + 4 * side), 16), 16)
+        cells = []
+        for chip in range(8):
+            mine, theirs = own_ref[chip, rows, :], other_ref[chip, rows, :]
+            cells.append(jnp.where(side == 0, mine, theirs))
+            cells.append(jnp.where(side == 0, theirs, mine))
+        place_windows(jnp.concatenate(cells, axis=1), windows_ref, 64 * x)
+
+    for step in range(ROWS * CELLS // WIDE):
         row, tile = step // (CELLS // WIDE), step % (CELLS // WIDE)
-        lanes = pl.ds(pl.multiple_of(tile * WIDE, WIDE), WIDE)
-        window = windows_ref[pl.ds(pl.multiple_of(row * 128, 128), 256), lanes]
+        lanes = slice(tile * WIDE, tile * WIDE + WIDE)
+        window = windows_ref[row * 128 : row * 128 + 256, lanes]
         pre = jnp.dot(fine_ref[...], window, preferred_element_type=F32)
         total = None
         for cell in range(8):
@@ -104,12 +105,9 @@
             act = value * gate
             slope_ref[row * 8 + cell, :, lanes] = gate + value * (1.0 - bent * bent)
             total = act if total is None else total + act
-        pooled_ref[pl.ds(pl.multiple_of(row * C1, C1), C1), lanes] = (
+        pooled_ref[row * C1 : row * C1 + C1, lanes] = (
             total.astype(F32) * (0.125 * 0.35)
         ).astype(BF16)
-        return 0
-
-    lax.fori_loop(0, ROWS * CELLS // WIDE, fine_step, 0)
 
     for tile in range(CELLS // TILE):
         lanes = slice(tile * TILE, tile * TILE + TILE)
@@ -146,10 +144,14 @@
     )
     for tap in range(9):
         both = grad[64 * tap : 64 * tap + 32, :192] + grad[64 * tap + 32 : 64 * tap + 64, 64:]
+        keep = jnp.where(side == 0, both[:16], both[16:])
+        send = jnp.where(side == 0, both[16:], both[:16])
         for dx in range(3):
             at = dx * 576 + tap * 64
-            grad_ref[:, at : at + 64] = both[:, 64 * dx : 64 * dx + 64]
-    grad_ref[:, 1728:1792] = jnp.zeros((32, 64), F32)
+            keep_ref[:, at : at + 64] = keep[:, 64 * dx : 64 * dx + 64]
+            send_ref[:, at : at + 64] = send[:, 64 * dx : 64 * dx + 64]
+    keep_ref[:, 1728:1792] = jnp.zeros((16, 64), F32)
+    send_ref[:, 1728:1792] = jnp.zeros((16, 64), F32)
 
     sum_ref[...] = jnp.zeros_like(sum_ref)
 
@@ -171,21 +173,23 @@
         total += jnp.dot(high, taps_ref[cell], preferred_element_type=F32)
         total += jnp.dot(low, taps_ref[cell], preferred_element_type=F32)
     total = total * (0.125 * 0.35)
-    for half in range(2):
-        for part in range(2):
-            at = 32 * half + 16 * part
-            grad_ref[16 * half : 16 * half + 16, 1792 + 128 * part : 1920 + 128 * part] = total[at : at + 16]
+    for part in range(4):
+        lanes = slice(1792 + 128 * part, 1920 + 128 * part)
+        keep_ref[:, lanes] = total[16 * part : 16 * part + 16]
+        send_ref[:, lanes] = total[16 * part : 16 * part + 16]
 
 
 def levels(side, own, other, fine, forward, backward, cot, taps):
     whole = pl.BlockSpec(memory_space=pltpu.VMEM)
     return pl.pallas_call(
         levels_kernel,
-        in_specs=[pl.BlockSpec(memory_space=pltpu.SMEM)] + [whole] * 7,
-        out_specs=[whole] * 2,
+        in_specs=[pl.BlockSpec(memory_space=pltpu.SMEM)]
+        + [whole] * 7,
+        out_specs=[whole] * 3,
         out_shape=[
             jax.ShapeDtypeStruct((64, CELLS), BF16),
-            jax.ShapeDtypeStruct((32, 2048), F32),
+            jax.ShapeDtypeStruct((16, SENT), F32),
+            jax.ShapeDtypeStruct((16, SENT), F32),
         ],
         scratch_shapes=[
             pltpu.VMEM((640, CELLS), BF16),
@@ -196,7 +200,7 @@
             pltpu.VMEM((ROWS * C1, CELLS), BF16),
             pltpu.VMEM((512, 256), F32),
         ],
-        compiler_params=pltpu.CompilerParams(vmem_limit_bytes=58 << 20),
+        compiler_params=pltpu.CompilerParams(vmem_limit_bytes=48 << 20),
         name="levels",
     )(side, own, other, fine, forward, backward, cot, taps)
 
@@ -211,32 +215,15 @@
     )
 
 
-def pair_list(target):
-    pairs = []
-    for gx in range(8):
-        for chip in range(8):
-            for core in range(2):
-                to_x, to_chip, to_core = target(gx, chip, core)
-                pairs.append(((gx * 8 + chip) * 2 + core, (to_x * 8 + to_chip % 8) * 2 + to_core))
-    return pairs
-
-
-def strip_parts(density, side):
+def strip_parts(density):
     sort = jnp.asarray(split_depth(), BF16)
     sorted_cells = jnp.dot(density.reshape(32, 1024), sort, preferred_element_type=F32).astype(BF16)
-    block = sorted_cells.reshape(C0, 8, 4, 256).transpose(1, 2, 0, 3).reshape(8, 16, 256)
-    kept = jnp.where(side == 0, block[:4], block[4:])
-    half = by_core(side, kept, swap(jnp.where(side == 0, block[4:], block[:4])), 2)
-    main = lax.ppermute(half, CHIP, pair_list(lambda gx, chip, core: (chip, gx, core)))
-    rim = lax.ppermute(
-        jnp.where(side == 0, half[:3], half[1:]),
-        CHIP,
-        pair_list(lambda gx, chip, core: (chip, gx + 2 * core - 1, 1 - core)),
-    )
-    part = jnp.concatenate([main, rim], 0).reshape(112, 512)
-    own = lax.all_to_all(jnp.broadcast_to(part[None], (8, 112, 512)), ("x", "zh"), 0, 0)
-    other = swap(jnp.where(side == 0, own[:, 16:64], own[:, :48]))
-    return own, other
+    block = sorted_cells.reshape(C0, 8, 4, 256).transpose(1, 2, 0, 3).reshape(128, 256)
+    column = lax.all_to_all(jnp.broadcast_to(block[None], (8, 128, 256)), ("x", "zh"), 0, 0)
+    strips = jnp.concatenate(
+        [jnp.roll(column[:, 80:], 1, 0), column, jnp.roll(column[:, :48], -1, 0)], axis=1
+    )
+    return lax.all_to_all(strips, ("zl", "y"), 0, 0)
 
 
 def coarse_weights(weight_two):
@@ -246,36 +233,43 @@
     return forward, forward.T
 
 
-def sum_grads(terms, side):
-    mine = jnp.where(side == 0, terms[:16], terms[16:])
-    mine = mine + swap(jnp.where(side == 0, terms[16:], terms[:16]))
-    copies = jnp.broadcast_to(mine.astype(BF16)[None], (8, 16, 2048))
-    summed = lax.all_to_all(copies, ("zl", "y"), 0, 0).astype(F32).sum(0)
-    copies = jnp.broadcast_to(summed[None, :, 1792:], (8, 16, 256))
-    one = lax.all_to_all(copies, ("x", "zh"), 0, 0).sum(0)
-    grad_two = by_core(side, summed[:, :1728], swap(summed[:, :1728]), 0)
-    one = by_core(side, one, swap(one), 0)
-    grad_one = one.reshape(2, 16, 2, 128).transpose(0, 2, 1, 3).reshape(C1, 128)[:, :108]
-    return grad_one, grad_two
+def sum_near(keep, send, features):
+    mine = (keep + swap(send)).astype(BF16)
+    copies = jnp.broadcast_to(mine[None], (8, 16, SENT))
+    terms, features = lax.optimization_barrier(
+        (lax.all_to_all(copies, ("zl", "y"), 0, 0), features)
+    )
+    return terms.astype(F32).sum(0), features
+
+
+def sum_far(copies):
+    one = lax.all_to_all(copies, ("x", "zh"), 0, 0).astype(F32).sum(0)
+    return one.reshape(16, 4, 128).transpose(1, 0, 2).reshape(C1, 128)[:, :108]
 
 
 def body(density, weight_one, weight_two, feature_cot):
     taps = jnp.asarray(window_taps(), BF16)
     side = lax.axis_index("core")
     with jax.named_scope("strip"):
-        own, other = strip_parts(density, side)
+        own = strip_parts(density)
     with jax.named_scope("weights"):
         fine_weight = jnp.einsum(
             "ok,srk->sor", jnp.pad(weight_one, ((0, 0), (0, 20))), taps, preferred_element_type=F32
         ).astype(BF16).reshape(512, 256)
         forward, backward = coarse_weights(weight_two)
         cot = feature_cot.transpose(1, 0, 2).reshape(64, CELLS)
-    features, terms = levels(
-        side.astype(jnp.int32).reshape(1), own, other, fine_weight, forward, backward, cot, taps
+    own, fine_weight, forward, backward, cot = lax.optimization_barrier(
+        (own, fine_weight, forward, backward, cot)
+    )
+    features, keep, send = levels(
+        side.astype(jnp.int32).reshape(1), own, swap(own), fine_weight, forward, backward, cot, taps
     )
     features = features.reshape(2, 32, CELLS).transpose(1, 0, 2)
     with jax.named_scope("sums"):
-        grad_one, grad_two = sum_grads(terms, side)
+        summed, features = sum_near(keep, send, features)
+        copies = jnp.broadcast_to(summed[None, :, 1792:].astype(BF16), (8, 16, 512))
+        grad_one = sum_far(copies)
+        grad_two = by_core(side, summed[:, :1728], swap(summed[:, :1728]), 0)
     return features, grad_one, grad_two
 
 

time: 110 us -> 97.8 us (0.89)
  starting transfers between devices: 30.9 us -> 15 us
  waiting for transfers between devices: 20.2 us -> 30.7 us
  Pallas kernels: 26.8 us -> 22.8 us
  local copies, waits for them, and re-layouts: 7.9 us -> 6.06 us
  other arithmetic: 3.21 us -> 1.95 us
    all_to_all x2 -> x3, waiting for transfers between devices: 16.8 us -> 27.4 us  [the longest x1 11.8 us: strip_parts(): return lax.all_to_all(strips, ('zl', 'y'), 0, 0)]
    ppermute x2 -> x0, starting transfers between devices: 7.35 us -> none  [the longest x1 6.69 us: strip_parts(): lax.ppermute(jnp.where(side == 0, half[:3], half[1:]), CHIP, pair_list(la...]
    all_to_all x2 -> x3, starting transfers between devices: 18.1 us -> 12.3 us  [the longest x1 4.65 us: strip_parts(): return lax.all_to_all(strips, ('zl', 'y'), 0, 0)]
    pallas_call x1, Pallas kernels: 26.8 us -> 22.8 us  [levels(): pl.pallas_call(levels_kernel, in_specs=[pl.BlockSpec(memory_space=pltpu.S...]
    ppermute x5 -> x3, starting transfers between devices: 5.42 us -> 2.64 us  [swap(): return lax.ppermute(values, 'core', [(0, 1), (1, 0)])]
    ppermute x2 -> x0, waiting for transfers between devices: 1.33 us -> none  [the longest x1 1.33 us: strip_parts(): lax.ppermute(jnp.where(side == 0, half[:3], half[1:]), CHIP, pair_list(la...]
    select_n x4 -> x0, other arithmetic: 1.18 us -> none  [the longest x1 1.04 us: sum_grads(): mine = mine + swap(jnp.where(side == 0, terms[16:], terms[:16]))]
    ppermute x5 -> x3, waiting for transfers between devices: 2.07 us -> 3.24 us  [swap(): return lax.ppermute(values, 'core', [(0, 1), (1, 0)])]
  transfers between devices with their start and end apart: 9 -> 6, of which waited for: 6 -> 5; matrix products, arithmetic and copies ran while one was open for 6% -> 5% of each run, Pallas kernels for 0% -> 0%
where the time goes in v3:
time: 97.8 us; the launch traced here: 97.1 us
  waiting for transfers between devices  30.7 us (31%)
  Pallas kernels  22.8 us (23%)
  blocking collectives  17.5 us (18%)
  starting transfers between devices  15 us (15%)
  local copies, waits for them, and re-layouts  6.06 us (6%)
  matrix products  2.34 us (2%)
  other arithmetic  1.95 us (2%)
    pallas_call x1, Pallas kernels, levels(): pl.pallas_call(levels_kernel, in_specs=[pl.BlockSpec(memory_space=pltpu.S...  22.8 us
    all_to_all x1, blocking collectives, strip_parts(): lax.all_to_all(jnp.broadcast_to(block[None], (8, 128, 256)), ('x', 'zh'),...  17.5 us
    all_to_all x1, waiting for transfers between devices, strip_parts(): return lax.all_to_all(strips, ('zl', 'y'), 0, 0)  11.8 us
    all_to_all x1, waiting for transfers between devices, sum_near(): lax.all_to_all(copies, ('zl', 'y'), 0, 0)  9.58 us
    all_to_all x1, waiting for transfers between devices, sum_far(): one = lax.all_to_all(copies, ('x', 'zh'), 0, 0).astype(F32).sum(0)  6.05 us
    all_to_all x1, starting transfers between devices, strip_parts(): return lax.all_to_all(strips, ('zl', 'y'), 0, 0)  4.65 us
    all_to_all x1, starting transfers between devices, sum_far(): one = lax.all_to_all(copies, ('x', 'zh'), 0, 0).astype(F32).sum(0)  4.15 us
    all_to_all x1, starting transfers between devices, sum_near(): lax.all_to_all(copies, ('zl', 'y'), 0, 0)  3.54 us
  transfers between devices with their start and end apart: 6, of which 5 were waited for; matrix products, arithmetic and copies ran while one was open for 5% of the time, Pallas kernels for 0%

profile of v3, /device:TPU:1, one launch (start us, length us, event | category | flops | bytes accessed | tf_op | source)
XLA Modules:
  0.0 97.1 jit_solution(14157709433837708732)
XLA Ops:
  0.6 0.0 copy-start
  0.6 0.8 copy-done
  1.5 2.1 %convolution_convert_fusion.1 = bf16[1024,32]{0,1:T(8,128)(2,1)S(1)} fusion(bf16[1024,1024]{1,0:T(8,128)(2,1)} %constant.15.clone, bf16[4,8,1024]{2,1,0:T(8,128)(2,1)S(1)} %copy-done), kind=kOutput, calls=%fused_computation.2 | convolution fusion | flops 67141632 | bytes 2228224 | tf_op jit(solution)/shard_map/strip/dot_general | solution.py:220
  3.5 0.1 copy.30
  3.7 17.5 %all_to_all.20 = bf16[8,128,256]{2,1,0:T(8,128)(2,1)S(1)} all-to-all(bf16[8,128,256]{2,1,0:T(8,128)(2,1)S(1)} %broadcast_in_dim.9), channel_id=1, replica_groups=mesh['x'=4,'zh'=2,'zl'=2,'y'=4,'core'=2] {'x','zh'}, dimensions={0} | all-to-all | bytes 1048576 | tf_op jit(solution)/shard_map/strip/all_to_all | solution.py:222
  21.2 0.0 copy-start.3
  21.3 1.0 %maximum_maximum_fusion = bf16[8,224,256]{2,1,0:T(8,128)(2,1)} fusion(bf16[1,48,256]{2,1,0:T(8,128)(2,1)S(1)} %get-tuple-element.24, bf16[7,48,256]{2,1,0:T(8,128)(2,1)S(1)} %get-tuple-element.26, bf16[8,128,256]{2,1,0:T(8,128)(2,1)S(1)} %all_to_all.20, bf16[7,48,256]{2,1,0:T(8,128)(2,1)S(1)} %get-tuple-element.25, bf16[1,48,256]{2,1,0:T(8,128)(2,1)S(1)} %get-tuple-element.23), kind=kLoop, calls=%fused_computation.3 | loop fusion | flops 4587520 | bytes 1835008 | tf_op jit(solution)/shard_map/strip/concatenate | solution.py:223
  22.2 4.6 %all-to-all-start.1 = ((bf16[8,224,256]{2,1,0:T(8,128)(2,1)}), bf16[8,224,256]{2,1,0:T(8,128)(2,1)S(1)}, u32[]{:S(2)}, u32[]{:S(2)}) async-start(bf16[8,224,256]{2,1,0:T(8,128)(2,1)} %maximum_maximum_fusion), calls=%async_computation.1 | async-start | bytes 1835008 | tf_op jit(solution)/shard_map/strip/all_to_all | solution.py:226
  26.9 0.0 copy-done.3
  26.9 0.2 reshape.45
  27.1 0.1 copy.38
  27.2 0.1 pad_bitcast_fusion.1
  27.3 0.0 copy-start.2
  27.3 0.1 maximum_bitcast_fusion
  27.4 0.0 copy-start.1
  27.5 0.0 copy-start.4
  27.5 0.3 copy.33
  27.8 0.4 reshape.46.forward_ref
  28.2 0.2 copy.34
  28.4 0.0 copy-done.2
  28.4 0.3 copy.35
  28.7 0.0 copy-done.1
  28.7 0.0 copy-done.4
  28.7 0.3 convolution_convert_fusion
  29.0 11.8 %all-to-all-done.1.own_ref = bf16[8,224,256]{2,1,0:T(8,128)(2,1)S(1)} async-done(((bf16[8,224,256]{2,1,0:T(8,128)(2,1)}), bf16[8,224,256]{2,1,0:T(8,128)(2,1)S(1)}, u32[]{:S(2)}, u32[]{:S(2)}) %all-to-all-start.1) | async-done | bytes 917536 | tf_op jit(solution)/shard_map/strip/all_to_all | solution.py:226
  40.8 1.3 %collective-permute-start = (bf16[8,224,256]{2,1,0:T(8,128)(2,1)S(1)}, bf16[8,224,256]{2,1,0:T(8,128)(2,1)}, u32[]{:S(2)}, u32[]{:S(2)}) collective-permute-start(bf16[8,224,256]{2,1,0:T(8,128)(2,1)S(1)} %all-to-all-done.1.own_ref), channel_id=1, source_target_pairs={{0,1},{1,0},{2,3},{3,2},{4,5},{5,4},{6,7},{7,6},{8,9},{9,8},{10,11... | collective-permute-start | bytes 2752520 | tf_op jit(solution)/shard_map/ppermute | solution.py:209
  42.1 2.2 %collective-permute-done.other_ref = bf16[8,224,256]{2,1,0:T(8,128)(2,1)} collective-permute-done((bf16[8,224,256]{2,1,0:T(8,128)(2,1)S(1)}, bf16[8,224,256]{2,1,0:T(8,128)(2,1)}, u32[]{:S(2)}, u32[]{:S(2)}) %collective-permute-start) | collective-permute-done | bytes 917536 | tf_op jit(solution)/shard_map/ppermute | solution.py:209
  44.4 22.8 %levels.1 = (bf16[64,4096]{1,0:T(8,128)(2,1)S(1)}, f32[16,2304]{1,0:T(8,128)S(1)}, f32[16,2304]{1,0:T(8,128)S(1)}) custom-call(s32[1]{0:T(128)} %bitcast.side_ref, bf16[8,224,256]{2,1,0:T(8,128)(2,1)S(1)} %all-to-all-done.1.own_ref, bf16[8,224,256]{2,1,0:T(8,128)(2,1)} %collective-permute-done.other_ref, bf16[512,256]{1,0:T(8,128)(2,1)S(1)} %bitcast.35, ...), custom_call_target="tpu_custom_call" | custom-call | tf_op jit(solution)/shard_map/levels/pallas_call | solution.py:184
  67.1 0.5 collective-permute-start.1
  67.6 1.0 %collective-permute-done.1 = f32[16,2304]{1,0:T(8,128)S(1)} collective-permute-done((f32[16,2304]{1,0:T(8,128)S(1)}, f32[16,2304]{1,0:T(8,128)S(1)}, u32[]{:S(2)}, u32[]{:S(2)}) %collective-permute-start.1) | collective-permute-done | bytes 147488 | tf_op jit(solution)/shard_map/sums/ppermute | solution.py:209
  68.6 0.9 broadcast_in_dim.10
  69.5 3.5 %all-to-all-start.2 = ((bf16[8,16,2304]{2,1,0:T(8,128)(2,1)}), bf16[8,16,2304]{2,1,0:T(8,128)(2,1)S(1)}, u32[]{:S(2)}, u32[]{:S(2)}) async-start(bf16[8,16,2304]{2,1,0:T(8,128)(2,1)} %broadcast_in_dim.10), calls=%async_computation.2 | async-start | bytes 1179648 | tf_op jit(solution)/shard_map/sums/all_to_all | solution.py:240
  73.0 1.3 %copy.41 = bf16[2,32,4096]{2,0,1:T(2,128)(2,1)} copy(bf16[2,32,4096]{2,1,0:T(8,128)(2,1)S(1)} %bitcast.36) | data formatting | bytes 1048576 | tf_op jit(solution)/shard_map/reshape | solution.py:267
  74.4 9.6 %all-to-all-done.2 = bf16[8,16,2304]{2,1,0:T(8,128)(2,1)S(1)} async-done(((bf16[8,16,2304]{2,1,0:T(8,128)(2,1)}), bf16[8,16,2304]{2,1,0:T(8,128)(2,1)S(1)}, u32[]{:S(2)}, u32[]{:S(2)}) %all-to-all-start.2) | async-done | bytes 589856 | tf_op jit(solution)/shard_map/sums/all_to_all | solution.py:240
  84.0 0.1 convert_reduce_fusion
  84.0 0.8 collective-permute-start.2
  84.9 0.7 broadcast_in_dim.22
  85.6 4.1 %all-to-all-start.3 = ((bf16[8,16,512]{2,1,0:T(8,128)(2,1)}), bf16[8,16,512]{2,1,0:T(8,128)(2,1)S(1)}, u32[]{:S(2)}, u32[]{:S(2)}) async-start(bf16[8,16,512]{2,1,0:T(8,128)(2,1)} %broadcast_in_dim.22), calls=%async_computation.3 | async-start | bytes 262144 | tf_op jit(solution)/shard_map/sums/all_to_all | solution.py:246
  89.7 0.0 collective-permute-done.2
  89.7 0.7 maximum_select_fusion
  90.4 6.0 %all-to-all-done.3 = bf16[8,16,512]{2,1,0:T(8,128)(2,1)S(1)} async-done(((bf16[8,16,512]{2,1,0:T(8,128)(2,1)}), bf16[8,16,512]{2,1,0:T(8,128)(2,1)S(1)}, u32[]{:S(2)}, u32[]{:S(2)}) %all-to-all-start.3) | async-done | bytes 131104 | tf_op jit(solution)/shard_map/sums/all_to_all | solution.py:246
  96.5 0.6 copy.37
  (9 shorter events, 0.2 us)
Async XLA Ops:
  0.6 0.8 copy-start
  21.2 5.6 %copy-start.3 = (bf16[32,1728]{1,0:T(8,128)(2,1)S(1)}, bf16[32,1728]{1,0:T(8,128)(2,1)}, u32[]{:S(2)}) copy-start(bf16[32,1728]{1,0:T(8,128)(2,1)} %param.8) | copy-start | bytes 331780
  22.2 18.5 %all-to-all-start.1 = ((bf16[8,224,256]{2,1,0:T(8,128)(2,1)}), bf16[8,224,256]{2,1,0:T(8,128)(2,1)S(1)}, u32[]{:S(2)}, u32[]{:S(2)}) async-start(bf16[8,224,256]{2,1,0:T(8,128)(2,1)} %maximum_maximum_fusion), calls=%async_computation.1 | async-start | bytes 1835008 | tf_op jit(solution)/shard_map/strip/all_to_all | solution.py:226
  27.3 1.1 %copy-start.2 = (bf16[32,2,4096]{2,1,0:T(2,128)(2,1)S(1)}, bf16[32,2,4096]{2,1,0:T(2,128)(2,1)}, u32[]{:S(2)}) copy-start(bf16[32,2,4096]{2,1,0:T(2,128)(2,1)} %param.9) | copy-start | bytes 1572868
  27.4 1.2 %copy-start.1 = (bf16[8,256,128]{2,1,0:T(8,128)(2,1)S(1)}, bf16[8,256,128]{2,1,0:T(8,128)(2,1)}, u32[]{:S(2)}) copy-start(bf16[8,256,128]{2,1,0:T(8,128)(2,1)} %constant.14.clone.taps_ref) | copy-start | bytes 1572868
  27.5 1.2 %copy-start.4 = (bf16[64,108]{1,0:T(8,128)(2,1)S(1)}, bf16[64,108]{1,0:T(8,128)(2,1)}, u32[]{:S(2)}) copy-start(bf16[64,108]{1,0:T(8,128)(2,1)} %param.7) | copy-start | bytes 41476
  40.8 3.6 %collective-permute-start = (bf16[8,224,256]{2,1,0:T(8,128)(2,1)S(1)}, bf16[8,224,256]{2,1,0:T(8,128)(2,1)}, u32[]{:S(2)}, u32[]{:S(2)}) collective-permute-start(bf16[8,224,256]{2,1,0:T(8,128)(2,1)S(1)} %all-to-all-done.1.own_ref), channel_id=1, source_target_pairs={{0,1},{1,0},{2,3},{3,2},{4,5},{5,4},{6,7},{7,6},{8,9},{9,8},{10,11... | collective-permute-start | bytes 2752520 | tf_op jit(solution)/shard_map/ppermute | solution.py:209
  67.1 1.5 %collective-permute-start.1 = (f32[16,2304]{1,0:T(8,128)S(1)}, f32[16,2304]{1,0:T(8,128)S(1)}, u32[]{:S(2)}, u32[]{:S(2)}) collective-permute-start(f32[16,2304]{1,0:T(8,128)S(1)} %get-tuple-element.19), channel_id=1, source_target_pairs={{0,1},{1,0},{2,3},{3,2},{4,5},{5,4},{6,7},{7,6},{8,9},{9,8},{10,11... | collective-permute-start | bytes 442376 | tf_op jit(solution)/shard_map/sums/ppermute | solution.py:209
  69.5 14.5 %all-to-all-start.2 = ((bf16[8,16,2304]{2,1,0:T(8,128)(2,1)}), bf16[8,16,2304]{2,1,0:T(8,128)(2,1)S(1)}, u32[]{:S(2)}, u32[]{:S(2)}) async-start(bf16[8,16,2304]{2,1,0:T(8,128)(2,1)} %broadcast_in_dim.10), calls=%async_computation.2 | async-start | bytes 1179648 | tf_op jit(solution)/shard_map/sums/all_to_all | solution.py:240
  84.0 5.7 %collective-permute-start.2 = (f32[16,1728]{1,0:T(8,128)S(1)}, f32[16,1728]{1,0:T(8,128)S(1)}, u32[]{:S(2)}, u32[]{:S(2)}) collective-permute-start(f32[16,1728]{1,0:T(8,128)S(1)} %slice.46), channel_id=1, source_target_pairs={{0,1},{1,0},{2,3},{3,2},{4,5},{5,4},{6,7},{7,6},{8,9},{9,8},{10,11... | collective-permute-start | bytes 331784 | tf_op jit(solution)/shard_map/sums/ppermute | solution.py:209
  85.6 10.9 %all-to-all-start.3 = ((bf16[8,16,512]{2,1,0:T(8,128)(2,1)}), bf16[8,16,512]{2,1,0:T(8,128)(2,1)S(1)}, u32[]{:S(2)}, u32[]{:S(2)}) async-start(bf16[8,16,512]{2,1,0:T(8,128)(2,1)} %broadcast_in_dim.22), calls=%async_computation.3 | async-start | bytes 262144 | tf_op jit(solution)/shard_map/sums/all_to_all | solution.py:246

commit v4 on v3

--- a/solution.py
+++ b/solution.py
@@ -14,7 +14,6 @@
 ROWS = 4
 TILE = 512
 WIDE = 2048
-SENT = 2304
 CHIP = ("x", "zh", "zl", "y", "core")
 F32 = jnp.float32
 BF16 = jnp.bfloat16
@@ -78,7 +77,7 @@
 
 def levels_kernel(
     side_ref, own_ref, other_ref, fine_ref, forward_ref, backward_ref, cot_ref, taps_ref,
-    feature_ref, keep_ref, send_ref,
+    feature_ref, keep_ref, send_ref, keep_one_ref, send_one_ref,
     windows_ref, slope_ref, pooled_ref, wide_ref, moved_ref, back_ref, sum_ref,
 ):
     side = side_ref[0]
@@ -150,9 +149,6 @@
             at = dx * 576 + tap * 64
             keep_ref[:, at : at + 64] = keep[:, 64 * dx : 64 * dx + 64]
             send_ref[:, at : at + 64] = send[:, 64 * dx : 64 * dx + 64]
-    keep_ref[:, 1728:1792] = jnp.zeros((16, 64), F32)
-    send_ref[:, 1728:1792] = jnp.zeros((16, 64), F32)
-
     sum_ref[...] = jnp.zeros_like(sum_ref)
 
     def back_step(row, _):
@@ -173,10 +169,8 @@
         total += jnp.dot(high, taps_ref[cell], preferred_element_type=F32)
         total += jnp.dot(low, taps_ref[cell], preferred_element_type=F32)
     total = total * (0.125 * 0.35)
-    for part in range(4):
-        lanes = slice(1792 + 128 * part, 1920 + 128 * part)
-        keep_ref[:, lanes] = total[16 * part : 16 * part + 16]
-        send_ref[:, lanes] = total[16 * part : 16 * part + 16]
+    keep_one_ref[...] = jnp.where(side == 0, total[:32], total[32:])
+    send_one_ref[...] = jnp.where(side == 0, total[32:], total[:32])
 
 
 def levels(side, own, other, fine, forward, backward, cot, taps):
@@ -185,11 +179,13 @@
         levels_kernel,
         in_specs=[pl.BlockSpec(memory_space=pltpu.SMEM)]
         + [whole] * 7,
-        out_specs=[whole] * 3,
+        out_specs=[whole] * 5,
         out_shape=[
             jax.ShapeDtypeStruct((64, CELLS), BF16),
-            jax.ShapeDtypeStruct((16, SENT), F32),
-            jax.ShapeDtypeStruct((16, SENT), F32),
+            jax.ShapeDtypeStruct((16, 1728), F32),
+            jax.ShapeDtypeStruct((16, 1728), F32),
+            jax.ShapeDtypeStruct((32, 128), F32),
+            jax.ShapeDtypeStruct((32, 128), F32),
         ],
         scratch_shapes=[
             pltpu.VMEM((640, CELLS), BF16),
@@ -233,18 +229,25 @@
     return forward, forward.T
 
 
-def sum_near(keep, send, features):
+def ring(count, step):
+    return [(i, (i + step) % count) for i in range(count)]
+
+
+def sum_one(keep, send, features, side):
     mine = (keep + swap(send)).astype(BF16)
-    copies = jnp.broadcast_to(mine[None], (8, 16, SENT))
-    terms, features = lax.optimization_barrier(
-        (lax.all_to_all(copies, ("zl", "y"), 0, 0), features)
-    )
-    return terms.astype(F32).sum(0), features
-
-
-def sum_far(copies):
-    one = lax.all_to_all(copies, ("x", "zh"), 0, 0).astype(F32).sum(0)
-    return one.reshape(16, 4, 128).transpose(1, 0, 2).reshape(C1, 128)[:, :108]
+    copies = jnp.broadcast_to(mine[None], (64, 32, 128))
+    terms = lax.all_to_all(copies, CHIP[:4], 0, 0)
+    terms, features = lax.optimization_barrier((terms, features))
+    half = terms.astype(F32).sum(0)
+    return by_core(side, half, swap(half), 0)[:, :108], features
+
+
+def sum_two(keep, send, side):
+    mine = (keep + swap(send)).astype(BF16)
+    mine = (mine.astype(F32) + lax.ppermute(mine, "zl", ring(2, 1)).astype(F32)).astype(BF16)
+    terms = [lax.ppermute(mine, "y", ring(4, step)).astype(F32) for step in range(1, 4)]
+    half = mine.astype(F32) + terms[0] + terms[1] + terms[2]
+    return by_core(side, half, swap(half), 0)
 
 
 def body(density, weight_one, weight_two, feature_cot):
@@ -261,15 +264,13 @@
     own, fine_weight, forward, backward, cot = lax.optimization_barrier(
         (own, fine_weight, forward, backward, cot)
     )
-    features, keep, send = levels(
+    features, keep, send, keep_one, send_one = levels(
         side.astype(jnp.int32).reshape(1), own, swap(own), fine_weight, forward, backward, cot, taps
     )
     features = features.reshape(2, 32, CELLS).transpose(1, 0, 2)
     with jax.named_scope("sums"):
-        summed, features = sum_near(keep, send, features)
-        copies = jnp.broadcast_to(summed[None, :, 1792:].astype(BF16), (8, 16, 512))
-        grad_one = sum_far(copies)
-        grad_two = by_core(side, summed[:, :1728], swap(summed[:, :1728]), 0)
+        grad_one, features = sum_one(keep_one, send_one, features, side)
+        grad_two = sum_two(keep, send, side)
     return features, grad_one, grad_two
 
 

time: 97.8 us -> 92.1 us (0.942)
  waiting for transfers between devices: 30.7 us -> 19.6 us
  starting transfers between devices: 15 us -> 21.1 us
  local copies, waits for them, and re-layouts: 6.06 us -> 4.76 us
    all_to_all x2 -> x1, waiting for transfers between devices: 15.6 us -> 0.01 us  [sum_one(): terms = lax.all_to_all(copies, CHIP[:4], 0, 0)]
    ppermute x0 -> x4, starting transfers between devices: none -> 5.01 us  [the longest x3 4.66 us: sum_two(): lax.ppermute(mine, 'y', ring(4, step)).astype(F32)]
    ppermute x0 -> x4, waiting for transfers between devices: none -> 4.65 us  [the longest x3 4.65 us: sum_two(): lax.ppermute(mine, 'y', ring(4, step)).astype(F32)]
    ppermute x3 -> x5, starting transfers between devices: 2.64 us -> 5.38 us  [swap(): return lax.ppermute(values, 'core', [(0, 1), (1, 0)])]
    all_to_all x2 -> x1, starting transfers between devices: 7.68 us -> 6.05 us  [sum_one(): terms = lax.all_to_all(copies, CHIP[:4], 0, 0)]
    ppermute x3 -> x5, waiting for transfers between devices: 3.24 us -> 3.2 us  [swap(): return lax.ppermute(values, 'core', [(0, 1), (1, 0)])]
  transfers between devices with their start and end apart: 6 -> 11, of which waited for: 5 -> 5; matrix products, arithmetic and copies ran while one was open for 5% -> 6% of each run, Pallas kernels for 0% -> 0%
where the time goes in v4:
time: 92.1 us; the launch traced here: 91.6 us
  Pallas kernels  22.8 us (25%)
  starting transfers between devices  21.1 us (23%)
  waiting for transfers between devices  19.6 us (21%)
  blocking collectives  17.5 us (19%)
  local copies, waits for them, and re-layouts  4.76 us (5%)
  other arithmetic  2.62 us (3%)
  matrix products  2.35 us (3%)
    pallas_call x1, Pallas kernels, levels(): pl.pallas_call(levels_kernel, in_specs=[pl.BlockSpec(memory_space=pltpu.S...  22.8 us
    all_to_all x1, blocking collectives, strip_parts(): lax.all_to_all(jnp.broadcast_to(block[None], (8, 128, 256)), ('x', 'zh'),...  17.5 us
    all_to_all x1, waiting for transfers between devices, strip_parts(): return lax.all_to_all(strips, ('zl', 'y'), 0, 0)  11.8 us
    all_to_all x1, starting transfers between devices, sum_one(): terms = lax.all_to_all(copies, CHIP[:4], 0, 0)  6.05 us
    ppermute x5, starting transfers between devices, swap(): return lax.ppermute(values, 'core', [(0, 1), (1, 0)])  5.38 us
    ppermute x3, starting transfers between devices, sum_two(): lax.ppermute(mine, 'y', ring(4, step)).astype(F32)  4.66 us
    all_to_all x1, starting transfers between devices, strip_parts(): return lax.all_to_all(strips, ('zl', 'y'), 0, 0)  4.65 us
    ppermute x3, waiting for transfers between devices, sum_two(): lax.ppermute(mine, 'y', ring(4, step)).astype(F32)  4.65 us
  transfers between devices with their start and end apart: 11, of which 5 were waited for; matrix products, arithmetic and copies ran while one was open for 6% of the time, Pallas kernels for 0%

profile of v4, /device:TPU:1, one launch (start us, length us, event | category | flops | bytes accessed | tf_op | source)
XLA Modules:
  0.0 91.6 jit_solution(382234140475313411)
XLA Ops:
  0.6 0.0 copy-start
  0.6 0.8 copy-done
  1.5 2.1 %convolution_convert_fusion.1 = bf16[1024,32]{0,1:T(8,128)(2,1)S(1)} fusion(bf16[1024,1024]{1,0:T(8,128)(2,1)} %constant.15.clone, bf16[4,8,1024]{2,1,0:T(8,128)(2,1)S(1)} %copy-done), kind=kOutput, calls=%fused_computation.1 | convolution fusion | flops 67141632 | bytes 2228224 | tf_op jit(solution)/shard_map/strip/dot_general | solution.py:216
  3.5 0.1 copy.22
  3.7 17.5 %all_to_all.15 = bf16[8,128,256]{2,1,0:T(8,128)(2,1)S(1)} all-to-all(bf16[8,128,256]{2,1,0:T(8,128)(2,1)S(1)} %broadcast_in_dim.14), channel_id=1, replica_groups=mesh['x'=4,'zh'=2,'zl'=2,'y'=4,'core'=2] {'x','zh'}, dimensions={0} | all-to-all | bytes 1048576 | tf_op jit(solution)/shard_map/strip/all_to_all | solution.py:218
  21.2 0.0 copy-start.3
  21.3 1.0 %maximum_maximum_fusion = bf16[8,224,256]{2,1,0:T(8,128)(2,1)} fusion(bf16[1,48,256]{2,1,0:T(8,128)(2,1)S(1)} %get-tuple-element.28, bf16[7,48,256]{2,1,0:T(8,128)(2,1)S(1)} %get-tuple-element.30, bf16[8,128,256]{2,1,0:T(8,128)(2,1)S(1)} %all_to_all.15, bf16[7,48,256]{2,1,0:T(8,128)(2,1)S(1)} %get-tuple-element.29, bf16[1,48,256]{2,1,0:T(8,128)(2,1)S(1)} %get-tuple-element.27), kind=kLoop, calls=%fused_computation.3 | loop fusion | flops 4587520 | bytes 1835008 | tf_op jit(solution)/shard_map/strip/concatenate | solution.py:219
  22.3 4.6 %all-to-all-start.1 = ((bf16[8,224,256]{2,1,0:T(8,128)(2,1)}), bf16[8,224,256]{2,1,0:T(8,128)(2,1)S(1)}, u32[]{:S(2)}, u32[]{:S(2)}) async-start(bf16[8,224,256]{2,1,0:T(8,128)(2,1)} %maximum_maximum_fusion), calls=%async_computation.1 | async-start | bytes 1835008 | tf_op jit(solution)/shard_map/strip/all_to_all | solution.py:222
  26.9 0.0 copy-done.3
  26.9 0.2 reshape.37
  27.1 0.1 copy.29
  27.2 0.1 pad_bitcast_fusion.1
  27.3 0.0 copy-start.2
  27.3 0.1 maximum_bitcast_fusion
  27.5 0.0 copy-start.1
  27.5 0.0 copy-start.4
  27.5 0.3 copy.25
  27.8 0.4 reshape.38.forward_ref
  28.2 0.2 copy.26
  28.4 0.0 copy-done.2
  28.4 0.3 copy.27
  28.7 0.0 copy-done.1
  28.7 0.0 copy-done.4
  28.7 0.3 convolution_convert_fusion
  29.0 11.8 %all-to-all-done.1.own_ref = bf16[8,224,256]{2,1,0:T(8,128)(2,1)S(1)} async-done(((bf16[8,224,256]{2,1,0:T(8,128)(2,1)}), bf16[8,224,256]{2,1,0:T(8,128)(2,1)S(1)}, u32[]{:S(2)}, u32[]{:S(2)}) %all-to-all-start.1) | async-done | bytes 917536 | tf_op jit(solution)/shard_map/strip/all_to_all | solution.py:222
  40.8 1.3 %collective-permute-start = (bf16[8,224,256]{2,1,0:T(8,128)(2,1)S(1)}, bf16[8,224,256]{2,1,0:T(8,128)(2,1)}, u32[]{:S(2)}, u32[]{:S(2)}) collective-permute-start(bf16[8,224,256]{2,1,0:T(8,128)(2,1)S(1)} %all-to-all-done.1.own_ref), channel_id=1, source_target_pairs={{0,1},{1,0},{2,3},{3,2},{4,5},{5,4},{6,7},{7,6},{8,9},{9,8},{10,11... | collective-permute-start | bytes 2752520 | tf_op jit(solution)/shard_map/ppermute | solution.py:205
  42.2 2.2 %collective-permute-done.other_ref = bf16[8,224,256]{2,1,0:T(8,128)(2,1)} collective-permute-done((bf16[8,224,256]{2,1,0:T(8,128)(2,1)S(1)}, bf16[8,224,256]{2,1,0:T(8,128)(2,1)}, u32[]{:S(2)}, u32[]{:S(2)}) %collective-permute-start) | collective-permute-done | bytes 917536 | tf_op jit(solution)/shard_map/ppermute | solution.py:205
  44.4 22.8 %levels.1 = (bf16[64,4096]{1,0:T(8,128)(2,1)S(1)}, f32[16,1728]{1,0:T(8,128)S(1)}, f32[16,1728]{1,0:T(8,128)S(1)}, f32[32,128]{1,0:T(8,128)S(1)}, f32[32,128]{1,0:T(8,128)S(1)}) custom-call(s32[1]{0:T(128)} %bitcast.side_ref, bf16[8,224,256]{2,1,0:T(8,128)(2,1)S(1)} %all-to-all-done.1.own_ref, bf16[8,224,256]{2,1,0:T(8,128)(2,1)} %collective-permute-done.other_ref, ...), custom_call_target="tpu_custom_call" | custom-call | tf_op jit(solution)/shard_map/levels/pallas_call | solution.py:178
  67.2 0.5 collective-permute-start.3
  67.6 0.1 collective-permute-start.1
  67.8 0.8 collective-permute-done.3
  68.6 0.4 collective-permute-start.4
  69.0 0.0 collective-permute-done.1
  69.0 0.9 broadcast_in_dim.15
  69.9 6.1 %all-to-all-start.2 = ((bf16[64,32,128]{2,1,0:T(8,128)(2,1)}), bf16[64,32,128]{2,1,0:T(8,128)(2,1)S(1)}, u32[]{:S(2)}, u32[]{:S(2)}) async-start(bf16[64,32,128]{2,1,0:T(8,128)(2,1)} %broadcast_in_dim.15), calls=%async_computation.2 | async-start | bytes 1048576 | tf_op jit(solution)/shard_map/sums/all_to_all | solution.py:239
  75.9 0.0 collective-permute-done.4
  76.0 1.1 %collective-permute-start.5 = (bf16[16,1728]{1,0:T(8,128)(2,1)S(1)}, bf16[16,1728]{1,0:T(8,128)(2,1)S(1)}, u32[]{:S(2)}, u32[]{:S(2)}) collective-permute-start(bf16[16,1728]{1,0:T(8,128)(2,1)S(1)} %add_convert_fusion), channel_id=1, source_target_pairs={{0,2},{2,4},{4,6},{6,0},{1,3},{3,5},{5,7},{7,1},{8,10},{10,12},{12... | collective-permute-start | bytes 165896 | tf_op jit(solution)/shard_map/sums/ppermute | solution.py:248
  77.0 2.4 %collective-permute-start.6 = (bf16[16,1728]{1,0:T(8,128)(2,1)S(1)}, bf16[16,1728]{1,0:T(8,128)(2,1)S(1)}, u32[]{:S(2)}, u32[]{:S(2)}) collective-permute-start(bf16[16,1728]{1,0:T(8,128)(2,1)S(1)} %add_convert_fusion), channel_id=1, source_target_pairs={{0,4},{2,6},{4,0},{6,2},{1,5},{3,7},{5,1},{7,3},{8,12},{10,14},{12... | collective-permute-start | bytes 165896 | tf_op jit(solution)/shard_map/sums/ppermute | solution.py:248
  79.4 1.2 %collective-permute-start.7 = (bf16[16,1728]{1,0:T(8,128)(2,1)S(1)}, bf16[16,1728]{1,0:T(8,128)(2,1)S(1)}, u32[]{:S(2)}, u32[]{:S(2)}) collective-permute-start(bf16[16,1728]{1,0:T(8,128)(2,1)S(1)} %add_convert_fusion), channel_id=1, source_target_pairs={{0,6},{2,0},{4,2},{6,4},{1,7},{3,1},{5,3},{7,5},{8,14},{10,8},{12,... | collective-permute-start | bytes 165896 | tf_op jit(solution)/shard_map/sums/ppermute | solution.py:248
  80.6 1.3 %copy.32 = bf16[2,32,4096]{2,0,1:T(2,128)(2,1)} copy(bf16[2,32,4096]{2,1,0:T(8,128)(2,1)S(1)} %bitcast.33) | data formatting | bytes 1048576 | tf_op jit(solution)/shard_map/reshape | solution.py:270
  81.9 0.0 collective-permute-done.5
  81.9 4.6 %collective-permute-done.6 = bf16[16,1728]{1,0:T(8,128)(2,1)S(1)} collective-permute-done((bf16[16,1728]{1,0:T(8,128)(2,1)S(1)}, bf16[16,1728]{1,0:T(8,128)(2,1)S(1)}, u32[]{:S(2)}, u32[]{:S(2)}) %collective-permute-start.6) | collective-permute-done | bytes 55328 | tf_op jit(solution)/shard_map/sums/ppermute | solution.py:248
  86.6 0.0 collective-permute-done.7
  86.6 1.8 %collective-permute-start.8 = (f32[16,1728]{1,0:T(8,128)S(1)}, f32[16,1728]{1,0:T(8,128)S(1)}, u32[]{:S(2)}, u32[]{:S(2)}) collective-permute-start(f32[16,1728]{1,0:T(8,128)S(1)} %convert_add_fusion), channel_id=1, source_target_pairs={{0,1},{1,0},{2,3},{3,2},{4,5},{5,4},{6,7},{7,6},{8,9},{9,8},{10,11... | collective-permute-start | bytes 331784 | tf_op jit(solution)/shard_map/sums/ppermute | solution.py:205
  88.5 0.0 all-to-all-done.2
  88.5 0.1 convert_reduce_fusion
  88.6 1.6 %collective-permute-start.2 = (f32[32,128]{1,0:T(8,128)S(1)}, f32[32,128]{1,0:T(8,128)S(1)}, u32[]{:S(2)}, u32[]{:S(2)}) collective-permute-start(f32[32,128]{1,0:T(8,128)S(1)} %convert_reduce_fusion), channel_id=1, source_target_pairs={{0,1},{1,0},{2,3},{3,2},{4,5},{5,4},{6,7},{7,6},{8,9},{9,8},{10,11... | collective-permute-start | bytes 49160 | tf_op jit(solution)/shard_map/sums/ppermute | solution.py:205
  90.2 0.0 collective-permute-done.8
  90.2 0.7 maximum_select_fusion
  90.9 0.1 collective-permute-done.2
  91.0 0.6 fusion.1
  (8 shorter events, 0.2 us)
Async XLA Ops:
  0.6 0.8 copy-start
  21.2 5.7 %copy-start.3 = (bf16[32,1728]{1,0:T(8,128)(2,1)S(1)}, bf16[32,1728]{1,0:T(8,128)(2,1)}, u32[]{:S(2)}) copy-start(bf16[32,1728]{1,0:T(8,128)(2,1)} %param.8) | copy-start | bytes 331780
  22.3 18.5 %all-to-all-start.1 = ((bf16[8,224,256]{2,1,0:T(8,128)(2,1)}), bf16[8,224,256]{2,1,0:T(8,128)(2,1)S(1)}, u32[]{:S(2)}, u32[]{:S(2)}) async-start(bf16[8,224,256]{2,1,0:T(8,128)(2,1)} %maximum_maximum_fusion), calls=%async_computation.1 | async-start | bytes 1835008 | tf_op jit(solution)/shard_map/strip/all_to_all | solution.py:222
  27.3 1.1 %copy-start.2 = (bf16[32,2,4096]{2,1,0:T(2,128)(2,1)S(1)}, bf16[32,2,4096]{2,1,0:T(2,128)(2,1)}, u32[]{:S(2)}) copy-start(bf16[32,2,4096]{2,1,0:T(2,128)(2,1)} %param.9) | copy-start | bytes 1572868
  27.5 1.2 %copy-start.1 = (bf16[8,256,128]{2,1,0:T(8,128)(2,1)S(1)}, bf16[8,256,128]{2,1,0:T(8,128)(2,1)}, u32[]{:S(2)}) copy-start(bf16[8,256,128]{2,1,0:T(8,128)(2,1)} %constant.14.clone.taps_ref) | copy-start | bytes 1572868
  27.5 1.2 %copy-start.4 = (bf16[64,108]{1,0:T(8,128)(2,1)S(1)}, bf16[64,108]{1,0:T(8,128)(2,1)}, u32[]{:S(2)}) copy-start(bf16[64,108]{1,0:T(8,128)(2,1)} %param.7) | copy-start | bytes 41476
  40.8 3.6 %collective-permute-start = (bf16[8,224,256]{2,1,0:T(8,128)(2,1)S(1)}, bf16[8,224,256]{2,1,0:T(8,128)(2,1)}, u32[]{:S(2)}, u32[]{:S(2)}) collective-permute-start(bf16[8,224,256]{2,1,0:T(8,128)(2,1)S(1)} %all-to-all-done.1.own_ref), channel_id=1, source_target_pairs={{0,1},{1,0},{2,3},{3,2},{4,5},{5,4},{6,7},{7,6},{8,9},{9,8},{10,11... | collective-permute-start | bytes 2752520 | tf_op jit(solution)/shard_map/ppermute | solution.py:205
  67.2 1.4 %collective-permute-start.3 = (f32[16,1728]{1,0:T(8,128)S(1)}, f32[16,1728]{1,0:T(8,128)S(1)}, u32[]{:S(2)}, u32[]{:S(2)}) collective-permute-start(f32[16,1728]{1,0:T(8,128)S(1)} %get-tuple-element.26), channel_id=1, source_target_pairs={{0,1},{1,0},{2,3},{3,2},{4,5},{5,4},{6,7},{7,6},{8,9},{9,8},{10,11... | collective-permute-start | bytes 331784 | tf_op jit(solution)/shard_map/sums/ppermute | solution.py:205
  67.6 1.3 %collective-permute-start.1 = (f32[32,128]{1,0:T(8,128)S(1)}, f32[32,128]{1,0:T(8,128)S(1)}, u32[]{:S(2)}, u32[]{:S(2)}) collective-permute-start(f32[32,128]{1,0:T(8,128)S(1)} %get-tuple-element.21), channel_id=1, source_target_pairs={{0,1},{1,0},{2,3},{3,2},{4,5},{5,4},{6,7},{7,6},{8,9},{9,8},{10,11... | collective-permute-start | bytes 49160 | tf_op jit(solution)/shard_map/sums/ppermute | solution.py:205
  68.6 7.3 %collective-permute-start.4 = (bf16[16,1728]{1,0:T(8,128)(2,1)S(1)}, bf16[16,1728]{1,0:T(8,128)(2,1)S(1)}, u32[]{:S(2)}, u32[]{:S(2)}) collective-permute-start(bf16[16,1728]{1,0:T(8,128)(2,1)S(1)} %add_convert_fusion.1), channel_id=1, source_target_pairs={{0,8},{8,0},{1,9},{9,1},{2,10},{10,2},{3,11},{11,3},{4,12},{12,4},... | collective-permute-start | bytes 165896 | tf_op jit(solution)/shard_map/sums/ppermute | solution.py:247
  69.9 18.6 %all-to-all-start.2 = ((bf16[64,32,128]{2,1,0:T(8,128)(2,1)}), bf16[64,32,128]{2,1,0:T(8,128)(2,1)S(1)}, u32[]{:S(2)}, u32[]{:S(2)}) async-start(bf16[64,32,128]{2,1,0:T(8,128)(2,1)} %broadcast_in_dim.15), calls=%async_computation.2 | async-start | bytes 1048576 | tf_op jit(solution)/shard_map/sums/all_to_all | solution.py:239
  76.0 6.0 %collective-permute-start.5 = (bf16[16,1728]{1,0:T(8,128)(2,1)S(1)}, bf16[16,1728]{1,0:T(8,128)(2,1)S(1)}, u32[]{:S(2)}, u32[]{:S(2)}) collective-permute-start(bf16[16,1728]{1,0:T(8,128)(2,1)S(1)} %add_convert_fusion), channel_id=1, source_target_pairs={{0,2},{2,4},{4,6},{6,0},{1,3},{3,5},{5,7},{7,1},{8,10},{10,12},{12... | collective-permute-start | bytes 165896 | tf_op jit(solution)/shard_map/sums/ppermute | solution.py:248
  77.0 9.6 %collective-permute-start.6 = (bf16[16,1728]{1,0:T(8,128)(2,1)S(1)}, bf16[16,1728]{1,0:T(8,128)(2,1)S(1)}, u32[]{:S(2)}, u32[]{:S(2)}) collective-permute-start(bf16[16,1728]{1,0:T(8,128)(2,1)S(1)} %add_convert_fusion), channel_id=1, source_target_pairs={{0,4},{2,6},{4,0},{6,2},{1,5},{3,7},{5,1},{7,3},{8,12},{10,14},{12... | collective-permute-start | bytes 165896 | tf_op jit(solution)/shard_map/sums/ppermute | solution.py:248
  79.4 7.2 %collective-permute-start.7 = (bf16[16,1728]{1,0:T(8,128)(2,1)S(1)}, bf16[16,1728]{1,0:T(8,128)(2,1)S(1)}, u32[]{:S(2)}, u32[]{:S(2)}) collective-permute-start(bf16[16,1728]{1,0:T(8,128)(2,1)S(1)} %add_convert_fusion), channel_id=1, source_target_pairs={{0,6},{2,0},{4,2},{6,4},{1,7},{3,1},{5,3},{7,5},{8,14},{10,8},{12,... | collective-permute-start | bytes 165896 | tf_op jit(solution)/shard_map/sums/ppermute | solution.py:248
  86.6 3.6 %collective-permute-start.8 = (f32[16,1728]{1,0:T(8,128)S(1)}, f32[16,1728]{1,0:T(8,128)S(1)}, u32[]{:S(2)}, u32[]{:S(2)}) collective-permute-start(f32[16,1728]{1,0:T(8,128)S(1)} %convert_add_fusion), channel_id=1, source_target_pairs={{0,1},{1,0},{2,3},{3,2},{4,5},{5,4},{6,7},{7,6},{8,9},{9,8},{10,11... | collective-permute-start | bytes 331784 | tf_op jit(solution)/shard_map/sums/ppermute | solution.py:205
  88.6 2.4 %collective-permute-start.2 = (f32[32,128]{1,0:T(8,128)S(1)}, f32[32,128]{1,0:T(8,128)S(1)}, u32[]{:S(2)}, u32[]{:S(2)}) collective-permute-start(f32[32,128]{1,0:T(8,128)S(1)} %convert_reduce_fusion), channel_id=1, source_target_pairs={{0,1},{1,0},{2,3},{3,2},{4,5},{5,4},{6,7},{7,6},{8,9},{9,8},{10,11... | collective-permute-start | bytes 49160 | tf_op jit(solution)/shard_map/sums/ppermute | solution.py:205

commit v5 on v4

--- a/solution.py
+++ b/solution.py
@@ -19,12 +19,31 @@
 BF16 = jnp.bfloat16
 
 
-def split_depth():
-    sort = np.zeros((1024, 1024), np.float32)
-    for y in range(16):
-        for z in range(Z):
-            sort[y * Z + z, ((y % 2) * 2 + z % 2) * 256 + (y // 2) * HZ + z // 2] = 1
-    return sort
+def iota(size, axis):
+    return lax.broadcasted_iota(jnp.int32, (size, size), axis)
+
+
+def sort_kernel(density_ref, copies_ref):
+    cells = jnp.concatenate([density_ref[i].astype(F32) for i in range(C0)], axis=0)
+    cells = jnp.concatenate([cells[:, :512], cells[:, 512:]], axis=0).astype(BF16)
+    y, z = iota(512, 0) // Z, iota(512, 0) % Z
+    lane = ((y % 2) * 2 + z % 2) * 128 + (y // 2) * HZ + z // 2
+    lanes = jnp.where(lane == iota(512, 1), 1.0, 0.0).astype(BF16)
+    sorted_cells = jnp.dot(cells, lanes, preferred_element_type=F32)
+    halves = [
+        jnp.concatenate(
+            [sorted_cells[32 * h : 32 * h + 32, 128 * p : 128 * p + 128] for p in range(4)], axis=0
+        )
+        for h in range(2)
+    ]
+    row = iota(128, 0)
+    source = row // C0 % 4 * 32 + row % C0 * 8 + row // 16
+    rows = jnp.where(source == iota(128, 1), 1.0, 0.0).astype(BF16)
+    block = jnp.dot(
+        rows, jnp.concatenate(halves, axis=1).astype(BF16), preferred_element_type=F32
+    ).astype(BF16)
+    for copy in range(8):
+        copies_ref[copy] = block
 
 
 def window_taps():
@@ -160,7 +179,7 @@
         )
         return 0
 
-    lax.fori_loop(0, ROWS, back_step, 0)
+    lax.fori_loop(0, ROWS, back_step, 0, unroll=2)
     total = jnp.zeros((C1, 128), F32)
     for cell in range(8):
         whole = sum_ref[C1 * cell : C1 * cell + C1, :]
@@ -212,10 +231,16 @@
 
 
 def strip_parts(density):
-    sort = jnp.asarray(split_depth(), BF16)
-    sorted_cells = jnp.dot(density.reshape(32, 1024), sort, preferred_element_type=F32).astype(BF16)
-    block = sorted_cells.reshape(C0, 8, 4, 256).transpose(1, 2, 0, 3).reshape(128, 256)
-    column = lax.all_to_all(jnp.broadcast_to(block[None], (8, 128, 256)), ("x", "zh"), 0, 0)
+    whole = pl.BlockSpec(memory_space=pltpu.VMEM)
+    copies = pl.pallas_call(
+        sort_kernel,
+        in_specs=[whole],
+        out_specs=whole,
+        out_shape=jax.ShapeDtypeStruct((8, 128, 256), BF16),
+        compiler_params=pltpu.CompilerParams(vmem_limit_bytes=8 << 20),
+        name="sort_block",
+    )(density)
+    column = lax.all_to_all(copies, ("x", "zh"), 0, 0)
     strips = jnp.concatenate(
         [jnp.roll(column[:, 80:], 1, 0), column, jnp.roll(column[:, :48], -1, 0)], axis=1
     )

time: 92.1 us -> 90.1 us (0.978)
  matrix products: 2.35 us -> 0.29 us
    dot_general x1 -> x0, matrix products: 2.05 us -> none  [strip_parts(): jnp.dot(density.reshape(32, 1024), sort, preferred_element_type=F32)]
where the time goes in v5:
time: 90.1 us; the launch traced here: 89.6 us
  Pallas kernels  22.9 us (25%)
  starting transfers between devices  21.2 us (24%)
  waiting for transfers between devices  19.1 us (21%)
  blocking collectives  17.5 us (19%)
  local copies, waits for them, and re-layouts  5.19 us (6%)
  other arithmetic  2.62 us (3%)
    pallas_call x1, Pallas kernels, levels(): pl.pallas_call(levels_kernel, in_specs=[pl.BlockSpec(memory_space=pltpu.S...  22.4 us
    all_to_all x1, blocking collectives, strip_parts(): column = lax.all_to_all(copies, ('x', 'zh'), 0, 0)  17.5 us
    all_to_all x1, waiting for transfers between devices, strip_parts(): return lax.all_to_all(strips, ('zl', 'y'), 0, 0)  11.3 us
    all_to_all x1, starting transfers between devices, sum_one(): terms = lax.all_to_all(copies, CHIP[:4], 0, 0)  6.06 us
    ppermute x5, starting transfers between devices, swap(): return lax.ppermute(values, 'core', [(0, 1), (1, 0)])  5.38 us
    all_to_all x1, starting transfers between devices, strip_parts(): return lax.all_to_all(strips, ('zl', 'y'), 0, 0)  4.78 us
    ppermute x3, starting transfers between devices, sum_two(): lax.ppermute(mine, 'y', ring(4, step)).astype(F32)  4.66 us
    ppermute x3, waiting for transfers between devices, sum_two(): lax.ppermute(mine, 'y', ring(4, step)).astype(F32)  4.65 us
  transfers between devices with their start and end apart: 11, of which 5 were waited for; matrix products, arithmetic and copies ran while one was open for 6% of the time, Pallas kernels for 0%

profile of v5, /device:TPU:1, one launch (start us, length us, event | category | flops | bytes accessed | tf_op | source)
XLA Modules:
  0.0 89.6 jit_solution(3833695617552837208)
XLA Ops:
  0.6 0.0 copy-start.1
  0.6 0.8 copy-done.1
  1.5 0.5 sort_block.1
  1.9 17.5 %all_to_all.15 = bf16[8,128,256]{2,1,0:T(8,128)(2,1)S(1)} all-to-all(bf16[8,128,256]{2,1,0:T(8,128)(2,1)S(1)} %sort_block.1), channel_id=1, replica_groups=mesh['x'=4,'zh'=2,'zl'=2,'y'=4,'core'=2] {'x','zh'}, dimensions={0} | all-to-all | bytes 1048576 | tf_op jit(solution)/shard_map/strip/all_to_all | solution.py:243
  19.5 1.0 %maximum_maximum_fusion = bf16[8,224,256]{2,1,0:T(8,128)(2,1)} fusion(bf16[1,48,256]{2,1,0:T(8,128)(2,1)S(1)} %get-tuple-element.28, bf16[7,48,256]{2,1,0:T(8,128)(2,1)S(1)} %get-tuple-element.30, bf16[8,128,256]{2,1,0:T(8,128)(2,1)S(1)} %all_to_all.15, bf16[7,48,256]{2,1,0:T(8,128)(2,1)S(1)} %get-tuple-element.29, bf16[1,48,256]{2,1,0:T(8,128)(2,1)S(1)} %get-tuple-element.27), kind=kLoop, calls=%fused_computation.2 | loop fusion | flops 4587520 | bytes 1835008 | tf_op jit(solution)/shard_map/strip/concatenate | solution.py:244
  20.5 0.0 copy-start.3
  20.5 4.8 %all-to-all-start.1 = ((bf16[8,224,256]{2,1,0:T(8,128)(2,1)}), bf16[8,224,256]{2,1,0:T(8,128)(2,1)S(1)}, u32[]{:S(2)}, u32[]{:S(2)}) async-start(bf16[8,224,256]{2,1,0:T(8,128)(2,1)} %maximum_maximum_fusion), calls=%async_computation.1 | async-start | bytes 1835008 | tf_op jit(solution)/shard_map/strip/all_to_all | solution.py:247
  25.3 0.0 copy-done.3
  25.3 0.2 reshape.27
  25.5 0.1 copy.25
  25.6 0.1 pad_bitcast_fusion.1
  25.7 0.1 maximum_bitcast_fusion
  25.8 0.3 copy.21
  26.2 0.0 copy-start.2
  26.2 0.4 reshape.28.forward_ref
  26.5 0.0 copy-start
  26.6 0.0 copy-start.4
  26.6 0.2 copy.22
  26.8 0.4 copy-done.2
  27.2 0.3 copy.23
  27.5 0.1 copy-done
  27.6 0.0 copy-done.4
  27.6 0.3 convolution_convert_fusion
  27.9 11.3 %all-to-all-done.1.own_ref = bf16[8,224,256]{2,1,0:T(8,128)(2,1)S(1)} async-done(((bf16[8,224,256]{2,1,0:T(8,128)(2,1)}), bf16[8,224,256]{2,1,0:T(8,128)(2,1)S(1)}, u32[]{:S(2)}, u32[]{:S(2)}) %all-to-all-start.1) | async-done | bytes 917536 | tf_op jit(solution)/shard_map/strip/all_to_all | solution.py:247
  39.2 1.3 %collective-permute-start = (bf16[8,224,256]{2,1,0:T(8,128)(2,1)S(1)}, bf16[8,224,256]{2,1,0:T(8,128)(2,1)}, u32[]{:S(2)}, u32[]{:S(2)}) collective-permute-start(bf16[8,224,256]{2,1,0:T(8,128)(2,1)S(1)} %all-to-all-done.1.own_ref), channel_id=1, source_target_pairs={{0,1},{1,0},{2,3},{3,2},{4,5},{5,4},{6,7},{7,6},{8,9},{9,8},{10,11... | collective-permute-start | bytes 2752520 | tf_op jit(solution)/shard_map/ppermute | solution.py:224
  40.6 2.2 %collective-permute-done.other_ref = bf16[8,224,256]{2,1,0:T(8,128)(2,1)} collective-permute-done((bf16[8,224,256]{2,1,0:T(8,128)(2,1)S(1)}, bf16[8,224,256]{2,1,0:T(8,128)(2,1)}, u32[]{:S(2)}, u32[]{:S(2)}) %collective-permute-start) | collective-permute-done | bytes 917536 | tf_op jit(solution)/shard_map/ppermute | solution.py:224
  42.8 22.4 %levels.1 = (bf16[64,4096]{1,0:T(8,128)(2,1)S(1)}, f32[16,1728]{1,0:T(8,128)S(1)}, f32[16,1728]{1,0:T(8,128)S(1)}, f32[32,128]{1,0:T(8,128)S(1)}, f32[32,128]{1,0:T(8,128)S(1)}) custom-call(s32[1]{0:T(128)} %bitcast.side_ref, bf16[8,224,256]{2,1,0:T(8,128)(2,1)S(1)} %all-to-all-done.1.own_ref, bf16[8,224,256]{2,1,0:T(8,128)(2,1)} %collective-permute-done.other_ref, ...), custom_call_target="tpu_custom_call" | custom-call | tf_op jit(solution)/shard_map/levels/pallas_call | solution.py:197
  65.2 0.5 collective-permute-start.3
  65.6 0.1 collective-permute-start.1
  65.8 0.8 collective-permute-done.3
  66.6 0.4 collective-permute-start.4
  67.0 0.0 collective-permute-done.1
  67.0 0.9 broadcast_in_dim.2
  67.9 6.1 %all-to-all-start.2 = ((bf16[64,32,128]{2,1,0:T(8,128)(2,1)}), bf16[64,32,128]{2,1,0:T(8,128)(2,1)S(1)}, u32[]{:S(2)}, u32[]{:S(2)}) async-start(bf16[64,32,128]{2,1,0:T(8,128)(2,1)} %broadcast_in_dim.2), calls=%async_computation.2 | async-start | bytes 1048576 | tf_op jit(solution)/shard_map/sums/all_to_all | solution.py:264
  73.9 0.0 collective-permute-done.4
  74.0 1.1 %collective-permute-start.5 = (bf16[16,1728]{1,0:T(8,128)(2,1)S(1)}, bf16[16,1728]{1,0:T(8,128)(2,1)S(1)}, u32[]{:S(2)}, u32[]{:S(2)}) collective-permute-start(bf16[16,1728]{1,0:T(8,128)(2,1)S(1)} %add_convert_fusion), channel_id=1, source_target_pairs={{0,2},{2,4},{4,6},{6,0},{1,3},{3,5},{5,7},{7,1},{8,10},{10,12},{12... | collective-permute-start | bytes 165896 | tf_op jit(solution)/shard_map/sums/ppermute | solution.py:273
  75.0 2.4 %collective-permute-start.6 = (bf16[16,1728]{1,0:T(8,128)(2,1)S(1)}, bf16[16,1728]{1,0:T(8,128)(2,1)S(1)}, u32[]{:S(2)}, u32[]{:S(2)}) collective-permute-start(bf16[16,1728]{1,0:T(8,128)(2,1)S(1)} %add_convert_fusion), channel_id=1, source_target_pairs={{0,4},{2,6},{4,0},{6,2},{1,5},{3,7},{5,1},{7,3},{8,12},{10,14},{12... | collective-permute-start | bytes 165896 | tf_op jit(solution)/shard_map/sums/ppermute | solution.py:273
  77.4 1.2 %collective-permute-start.7 = (bf16[16,1728]{1,0:T(8,128)(2,1)S(1)}, bf16[16,1728]{1,0:T(8,128)(2,1)S(1)}, u32[]{:S(2)}, u32[]{:S(2)}) collective-permute-start(bf16[16,1728]{1,0:T(8,128)(2,1)S(1)} %add_convert_fusion), channel_id=1, source_target_pairs={{0,6},{2,0},{4,2},{6,4},{1,7},{3,1},{5,3},{7,5},{8,14},{10,8},{12,... | collective-permute-start | bytes 165896 | tf_op jit(solution)/shard_map/sums/ppermute | solution.py:273
  78.6 1.3 %copy.28 = bf16[2,32,4096]{2,0,1:T(2,128)(2,1)} copy(bf16[2,32,4096]{2,1,0:T(8,128)(2,1)S(1)} %bitcast.24) | data formatting | bytes 1048576 | tf_op jit(solution)/shard_map/reshape | solution.py:295
  80.0 0.0 collective-permute-done.5
  80.0 4.6 %collective-permute-done.6 = bf16[16,1728]{1,0:T(8,128)(2,1)S(1)} collective-permute-done((bf16[16,1728]{1,0:T(8,128)(2,1)S(1)}, bf16[16,1728]{1,0:T(8,128)(2,1)S(1)}, u32[]{:S(2)}, u32[]{:S(2)}) %collective-permute-start.6) | collective-permute-done | bytes 55328 | tf_op jit(solution)/shard_map/sums/ppermute | solution.py:273
  84.6 0.0 collective-permute-done.7
  84.6 1.8 %collective-permute-start.8 = (f32[16,1728]{1,0:T(8,128)S(1)}, f32[16,1728]{1,0:T(8,128)S(1)}, u32[]{:S(2)}, u32[]{:S(2)}) collective-permute-start(f32[16,1728]{1,0:T(8,128)S(1)} %convert_add_fusion), channel_id=1, source_target_pairs={{0,1},{1,0},{2,3},{3,2},{4,5},{5,4},{6,7},{7,6},{8,9},{9,8},{10,11... | collective-permute-start | bytes 331784 | tf_op jit(solution)/shard_map/sums/ppermute | solution.py:224
  86.5 0.0 all-to-all-done.2
  86.5 0.1 convert_reduce_fusion
  86.6 1.6 %collective-permute-start.2 = (f32[32,128]{1,0:T(8,128)S(1)}, f32[32,128]{1,0:T(8,128)S(1)}, u32[]{:S(2)}, u32[]{:S(2)}) collective-permute-start(f32[32,128]{1,0:T(8,128)S(1)} %convert_reduce_fusion), channel_id=1, source_target_pairs={{0,1},{1,0},{2,3},{3,2},{4,5},{5,4},{6,7},{7,6},{8,9},{9,8},{10,11... | collective-permute-start | bytes 49160 | tf_op jit(solution)/shard_map/sums/ppermute | solution.py:224
  88.2 0.0 collective-permute-done.8
  88.2 0.7 maximum_select_fusion
  88.9 0.1 collective-permute-done.2
  89.0 0.6 fusion
  (6 shorter events, 0.1 us)
Async XLA Ops:
  0.6 0.8 copy-start.1
  20.5 4.8 %copy-start.3 = (bf16[32,1728]{1,0:T(8,128)(2,1)S(1)}, bf16[32,1728]{1,0:T(8,128)(2,1)}, u32[]{:S(2)}) copy-start(bf16[32,1728]{1,0:T(8,128)(2,1)} %param.7) | copy-start | bytes 331780
  20.5 18.7 %all-to-all-start.1 = ((bf16[8,224,256]{2,1,0:T(8,128)(2,1)}), bf16[8,224,256]{2,1,0:T(8,128)(2,1)S(1)}, u32[]{:S(2)}, u32[]{:S(2)}) async-start(bf16[8,224,256]{2,1,0:T(8,128)(2,1)} %maximum_maximum_fusion), calls=%async_computation.1 | async-start | bytes 1835008 | tf_op jit(solution)/shard_map/strip/all_to_all | solution.py:247
  26.2 1.0 %copy-start.2 = (bf16[32,2,4096]{2,1,0:T(2,128)(2,1)S(1)}, bf16[32,2,4096]{2,1,0:T(2,128)(2,1)}, u32[]{:S(2)}) copy-start(bf16[32,2,4096]{2,1,0:T(2,128)(2,1)} %param.8) | copy-start | bytes 1572868
  26.5 1.1 %copy-start = (bf16[8,256,128]{2,1,0:T(8,128)(2,1)S(1)}, bf16[8,256,128]{2,1,0:T(8,128)(2,1)}, u32[]{:S(2)}) copy-start(bf16[8,256,128]{2,1,0:T(8,128)(2,1)} %constant.12.clone.taps_ref) | copy-start | bytes 1572868
  26.6 1.1 %copy-start.4 = (bf16[64,108]{1,0:T(8,128)(2,1)S(1)}, bf16[64,108]{1,0:T(8,128)(2,1)}, u32[]{:S(2)}) copy-start(bf16[64,108]{1,0:T(8,128)(2,1)} %param.6) | copy-start | bytes 41476
  39.2 3.6 %collective-permute-start = (bf16[8,224,256]{2,1,0:T(8,128)(2,1)S(1)}, bf16[8,224,256]{2,1,0:T(8,128)(2,1)}, u32[]{:S(2)}, u32[]{:S(2)}) collective-permute-start(bf16[8,224,256]{2,1,0:T(8,128)(2,1)S(1)} %all-to-all-done.1.own_ref), channel_id=1, source_target_pairs={{0,1},{1,0},{2,3},{3,2},{4,5},{5,4},{6,7},{7,6},{8,9},{9,8},{10,11... | collective-permute-start | bytes 2752520 | tf_op jit(solution)/shard_map/ppermute | solution.py:224
  65.2 1.4 %collective-permute-start.3 = (f32[16,1728]{1,0:T(8,128)S(1)}, f32[16,1728]{1,0:T(8,128)S(1)}, u32[]{:S(2)}, u32[]{:S(2)}) collective-permute-start(f32[16,1728]{1,0:T(8,128)S(1)} %get-tuple-element.26), channel_id=1, source_target_pairs={{0,1},{1,0},{2,3},{3,2},{4,5},{5,4},{6,7},{7,6},{8,9},{9,8},{10,11... | collective-permute-start | bytes 331784 | tf_op jit(solution)/shard_map/sums/ppermute | solution.py:224
  65.6 1.3 %collective-permute-start.1 = (f32[32,128]{1,0:T(8,128)S(1)}, f32[32,128]{1,0:T(8,128)S(1)}, u32[]{:S(2)}, u32[]{:S(2)}) collective-permute-start(f32[32,128]{1,0:T(8,128)S(1)} %get-tuple-element.21), channel_id=1, source_target_pairs={{0,1},{1,0},{2,3},{3,2},{4,5},{5,4},{6,7},{7,6},{8,9},{9,8},{10,11... | collective-permute-start | bytes 49160 | tf_op jit(solution)/shard_map/sums/ppermute | solution.py:224
  66.6 7.3 %collective-permute-start.4 = (bf16[16,1728]{1,0:T(8,128)(2,1)S(1)}, bf16[16,1728]{1,0:T(8,128)(2,1)S(1)}, u32[]{:S(2)}, u32[]{:S(2)}) collective-permute-start(bf16[16,1728]{1,0:T(8,128)(2,1)S(1)} %add_convert_fusion.1), channel_id=1, source_target_pairs={{0,8},{8,0},{1,9},{9,1},{2,10},{10,2},{3,11},{11,3},{4,12},{12,4},... | collective-permute-start | bytes 165896 | tf_op jit(solution)/shard_map/sums/ppermute | solution.py:272
  67.9 18.6 %all-to-all-start.2 = ((bf16[64,32,128]{2,1,0:T(8,128)(2,1)}), bf16[64,32,128]{2,1,0:T(8,128)(2,1)S(1)}, u32[]{:S(2)}, u32[]{:S(2)}) async-start(bf16[64,32,128]{2,1,0:T(8,128)(2,1)} %broadcast_in_dim.2), calls=%async_computation.2 | async-start | bytes 1048576 | tf_op jit(solution)/shard_map/sums/all_to_all | solution.py:264
  74.0 6.0 %collective-permute-start.5 = (bf16[16,1728]{1,0:T(8,128)(2,1)S(1)}, bf16[16,1728]{1,0:T(8,128)(2,1)S(1)}, u32[]{:S(2)}, u32[]{:S(2)}) collective-permute-start(bf16[16,1728]{1,0:T(8,128)(2,1)S(1)} %add_convert_fusion), channel_id=1, source_target_pairs={{0,2},{2,4},{4,6},{6,0},{1,3},{3,5},{5,7},{7,1},{8,10},{10,12},{12... | collective-permute-start | bytes 165896 | tf_op jit(solution)/shard_map/sums/ppermute | solution.py:273
  75.0 9.6 %collective-permute-start.6 = (bf16[16,1728]{1,0:T(8,128)(2,1)S(1)}, bf16[16,1728]{1,0:T(8,128)(2,1)S(1)}, u32[]{:S(2)}, u32[]{:S(2)}) collective-permute-start(bf16[16,1728]{1,0:T(8,128)(2,1)S(1)} %add_convert_fusion), channel_id=1, source_target_pairs={{0,4},{2,6},{4,0},{6,2},{1,5},{3,7},{5,1},{7,3},{8,12},{10,14},{12... | collective-permute-start | bytes 165896 | tf_op jit(solution)/shard_map/sums/ppermute | solution.py:273
  77.4 7.2 %collective-permute-start.7 = (bf16[16,1728]{1,0:T(8,128)(2,1)S(1)}, bf16[16,1728]{1,0:T(8,128)(2,1)S(1)}, u32[]{:S(2)}, u32[]{:S(2)}) collective-permute-start(bf16[16,1728]{1,0:T(8,128)(2,1)S(1)} %add_convert_fusion), channel_id=1, source_target_pairs={{0,6},{2,0},{4,2},{6,4},{1,7},{3,1},{5,3},{7,5},{8,14},{10,8},{12,... | collective-permute-start | bytes 165896 | tf_op jit(solution)/shard_map/sums/ppermute | solution.py:273
  84.6 3.6 %collective-permute-start.8 = (f32[16,1728]{1,0:T(8,128)S(1)}, f32[16,1728]{1,0:T(8,128)S(1)}, u32[]{:S(2)}, u32[]{:S(2)}) collective-permute-start(f32[16,1728]{1,0:T(8,128)S(1)} %convert_add_fusion), channel_id=1, source_target_pairs={{0,1},{1,0},{2,3},{3,2},{4,5},{5,4},{6,7},{7,6},{8,9},{9,8},{10,11... | collective-permute-start | bytes 331784 | tf_op jit(solution)/shard_map/sums/ppermute | solution.py:224
  86.6 2.4 %collective-permute-start.2 = (f32[32,128]{1,0:T(8,128)S(1)}, f32[32,128]{1,0:T(8,128)S(1)}, u32[]{:S(2)}, u32[]{:S(2)}) collective-permute-start(f32[32,128]{1,0:T(8,128)S(1)} %convert_reduce_fusion), channel_id=1, source_target_pairs={{0,1},{1,0},{2,3},{3,2},{4,5},{5,4},{6,7},{7,6},{8,9},{9,8},{10,11... | collective-permute-start | bytes 49160 | tf_op jit(solution)/shard_map/sums/ppermute | solution.py:224

commit v6 on v5

--- a/solution.py
+++ b/solution.py
@@ -270,7 +270,7 @@
 def sum_two(keep, send, side):
     mine = (keep + swap(send)).astype(BF16)
     mine = (mine.astype(F32) + lax.ppermute(mine, "zl", ring(2, 1)).astype(F32)).astype(BF16)
-    terms = [lax.ppermute(mine, "y", ring(4, step)).astype(F32) for step in range(1, 4)]
+    terms = [lax.ppermute(mine, "y", ring(4, step)).astype(F32) for step in (2, 1, 3)]
     half = mine.astype(F32) + terms[0] + terms[1] + terms[2]
     return by_core(side, half, swap(half), 0)
 

time: 90.1 us -> 90.1 us (level)
  no operation moved by 1% of the time
where the time goes in v6:
time: 90.1 us; the launch traced here: 89.6 us
  Pallas kernels  22.9 us (25%)
  starting transfers between devices  21.1 us (23%)
  waiting for transfers between devices  19.3 us (21%)
  blocking collectives  17.5 us (19%)
  local copies, waits for them, and re-layouts  5.19 us (6%)
  other arithmetic  2.62 us (3%)
    pallas_call x1, Pallas kernels, levels(): pl.pallas_call(levels_kernel, in_specs=[pl.BlockSpec(memory_space=pltpu.S...  22.4 us
    all_to_all x1, blocking collectives, strip_parts(): column = lax.all_to_all(copies, ('x', 'zh'), 0, 0)  17.5 us
    all_to_all x1, waiting for transfers between devices, strip_parts(): return lax.all_to_all(strips, ('zl', 'y'), 0, 0)  11.3 us
    all_to_all x1, starting transfers between devices, sum_one(): terms = lax.all_to_all(copies, CHIP[:4], 0, 0)  6.06 us
    ppermute x3, starting transfers between devices, sum_two(): lax.ppermute(mine, 'y', ring(4, step)).astype(F32)  5.27 us
    ppermute x3, waiting for transfers between devices, sum_two(): lax.ppermute(mine, 'y', ring(4, step)).astype(F32)  4.83 us
    all_to_all x1, starting transfers between devices, strip_parts(): return lax.all_to_all(strips, ('zl', 'y'), 0, 0)  4.78 us
    ppermute x5, starting transfers between devices, swap(): return lax.ppermute(values, 'core', [(0, 1), (1, 0)])  4.59 us
  transfers between devices with their start and end apart: 11, of which 5 were waited for; matrix products, arithmetic and copies ran while one was open for 6% of the time, Pallas kernels for 0%

profile of v6, /device:TPU:1, one launch (start us, length us, event | category | flops | bytes accessed | tf_op | source)
XLA Modules:
  0.0 89.6 jit_solution(10733811736337994615)
XLA Ops:
  0.6 0.0 copy-start.1
  0.6 0.8 copy-done.1
  1.5 0.5 sort_block.1
  1.9 17.5 %all_to_all.15 = bf16[8,128,256]{2,1,0:T(8,128)(2,1)S(1)} all-to-all(bf16[8,128,256]{2,1,0:T(8,128)(2,1)S(1)} %sort_block.1), channel_id=1, replica_groups=mesh['x'=4,'zh'=2,'zl'=2,'y'=4,'core'=2] {'x','zh'}, dimensions={0} | all-to-all | bytes 1048576 | tf_op jit(solution)/shard_map/strip/all_to_all | solution.py:243
  19.5 1.0 %maximum_maximum_fusion = bf16[8,224,256]{2,1,0:T(8,128)(2,1)} fusion(bf16[1,48,256]{2,1,0:T(8,128)(2,1)S(1)} %get-tuple-element.28, bf16[7,48,256]{2,1,0:T(8,128)(2,1)S(1)} %get-tuple-element.30, bf16[8,128,256]{2,1,0:T(8,128)(2,1)S(1)} %all_to_all.15, bf16[7,48,256]{2,1,0:T(8,128)(2,1)S(1)} %get-tuple-element.29, bf16[1,48,256]{2,1,0:T(8,128)(2,1)S(1)} %get-tuple-element.27), kind=kLoop, calls=%fused_computation.2 | loop fusion | flops 4587520 | bytes 1835008 | tf_op jit(solution)/shard_map/strip/concatenate | solution.py:244
  20.5 0.0 copy-start.3
  20.5 4.8 %all-to-all-start.1 = ((bf16[8,224,256]{2,1,0:T(8,128)(2,1)}), bf16[8,224,256]{2,1,0:T(8,128)(2,1)S(1)}, u32[]{:S(2)}, u32[]{:S(2)}) async-start(bf16[8,224,256]{2,1,0:T(8,128)(2,1)} %maximum_maximum_fusion), calls=%async_computation.1 | async-start | bytes 1835008 | tf_op jit(solution)/shard_map/strip/all_to_all | solution.py:247
  25.3 0.0 copy-done.3
  25.3 0.2 reshape.27
  25.5 0.1 copy.25
  25.6 0.1 pad_bitcast_fusion.1
  25.7 0.1 maximum_bitcast_fusion
  25.8 0.3 copy.21
  26.2 0.0 copy-start.2
  26.2 0.4 reshape.28.forward_ref
  26.5 0.0 copy-start
  26.6 0.0 copy-start.4
  26.6 0.2 copy.22
  26.8 0.4 copy-done.2
  27.2 0.3 copy.23
  27.5 0.1 copy-done
  27.6 0.0 copy-done.4
  27.6 0.3 convolution_convert_fusion
  27.9 11.3 %all-to-all-done.1.own_ref = bf16[8,224,256]{2,1,0:T(8,128)(2,1)S(1)} async-done(((bf16[8,224,256]{2,1,0:T(8,128)(2,1)}), bf16[8,224,256]{2,1,0:T(8,128)(2,1)S(1)}, u32[]{:S(2)}, u32[]{:S(2)}) %all-to-all-start.1) | async-done | bytes 917536 | tf_op jit(solution)/shard_map/strip/all_to_all | solution.py:247
  39.2 1.3 %collective-permute-start = (bf16[8,224,256]{2,1,0:T(8,128)(2,1)S(1)}, bf16[8,224,256]{2,1,0:T(8,128)(2,1)}, u32[]{:S(2)}, u32[]{:S(2)}) collective-permute-start(bf16[8,224,256]{2,1,0:T(8,128)(2,1)S(1)} %all-to-all-done.1.own_ref), channel_id=1, source_target_pairs={{0,1},{1,0},{2,3},{3,2},{4,5},{5,4},{6,7},{7,6},{8,9},{9,8},{10,11... | collective-permute-start | bytes 2752520 | tf_op jit(solution)/shard_map/ppermute | solution.py:224
  40.6 2.2 %collective-permute-done.other_ref = bf16[8,224,256]{2,1,0:T(8,128)(2,1)} collective-permute-done((bf16[8,224,256]{2,1,0:T(8,128)(2,1)S(1)}, bf16[8,224,256]{2,1,0:T(8,128)(2,1)}, u32[]{:S(2)}, u32[]{:S(2)}) %collective-permute-start) | collective-permute-done | bytes 917536 | tf_op jit(solution)/shard_map/ppermute | solution.py:224
  42.8 22.4 %levels.1 = (bf16[64,4096]{1,0:T(8,128)(2,1)S(1)}, f32[16,1728]{1,0:T(8,128)S(1)}, f32[16,1728]{1,0:T(8,128)S(1)}, f32[32,128]{1,0:T(8,128)S(1)}, f32[32,128]{1,0:T(8,128)S(1)}) custom-call(s32[1]{0:T(128)} %bitcast.side_ref, bf16[8,224,256]{2,1,0:T(8,128)(2,1)S(1)} %all-to-all-done.1.own_ref, bf16[8,224,256]{2,1,0:T(8,128)(2,1)} %collective-permute-done.other_ref, ...), custom_call_target="tpu_custom_call" | custom-call | tf_op jit(solution)/shard_map/levels/pallas_call | solution.py:197
  65.2 0.5 collective-permute-start.3
  65.6 0.1 collective-permute-start.1
  65.8 0.8 collective-permute-done.3
  66.6 0.4 collective-permute-start.4
  67.0 0.0 collective-permute-done.1
  67.0 0.9 broadcast_in_dim.2
  67.9 6.1 %all-to-all-start.2 = ((bf16[64,32,128]{2,1,0:T(8,128)(2,1)}), bf16[64,32,128]{2,1,0:T(8,128)(2,1)S(1)}, u32[]{:S(2)}, u32[]{:S(2)}) async-start(bf16[64,32,128]{2,1,0:T(8,128)(2,1)} %broadcast_in_dim.2), calls=%async_computation.2 | async-start | bytes 1048576 | tf_op jit(solution)/shard_map/sums/all_to_all | solution.py:264
  73.9 0.0 collective-permute-done.4
  74.0 2.6 %collective-permute-start.5 = (bf16[16,1728]{1,0:T(8,128)(2,1)S(1)}, bf16[16,1728]{1,0:T(8,128)(2,1)S(1)}, u32[]{:S(2)}, u32[]{:S(2)}) collective-permute-start(bf16[16,1728]{1,0:T(8,128)(2,1)S(1)} %add_convert_fusion), channel_id=1, source_target_pairs={{0,4},{2,6},{4,0},{6,2},{1,5},{3,7},{5,1},{7,3},{8,12},{10,14},{12... | collective-permute-start | bytes 165896 | tf_op jit(solution)/shard_map/sums/ppermute | solution.py:273
  76.6 0.3 collective-permute-start.6
  76.8 2.4 %collective-permute-start.7 = (bf16[16,1728]{1,0:T(8,128)(2,1)S(1)}, bf16[16,1728]{1,0:T(8,128)(2,1)S(1)}, u32[]{:S(2)}, u32[]{:S(2)}) collective-permute-start(bf16[16,1728]{1,0:T(8,128)(2,1)S(1)} %add_convert_fusion), channel_id=1, source_target_pairs={{0,6},{2,0},{4,2},{6,4},{1,7},{3,1},{5,3},{7,5},{8,14},{10,8},{12,... | collective-permute-start | bytes 165896 | tf_op jit(solution)/shard_map/sums/ppermute | solution.py:273
  79.2 1.3 %copy.28 = bf16[2,32,4096]{2,0,1:T(2,128)(2,1)} copy(bf16[2,32,4096]{2,1,0:T(8,128)(2,1)S(1)} %bitcast.24) | data formatting | bytes 1048576 | tf_op jit(solution)/shard_map/reshape | solution.py:295
  80.6 0.0 collective-permute-done.5
  80.6 4.8 %collective-permute-done.6 = bf16[16,1728]{1,0:T(8,128)(2,1)S(1)} collective-permute-done((bf16[16,1728]{1,0:T(8,128)(2,1)S(1)}, bf16[16,1728]{1,0:T(8,128)(2,1)S(1)}, u32[]{:S(2)}, u32[]{:S(2)}) %collective-permute-start.6) | collective-permute-done | bytes 55328 | tf_op jit(solution)/shard_map/sums/ppermute | solution.py:273
  85.4 0.0 collective-permute-done.7
  85.4 0.7 collective-permute-start.8
  86.1 0.0 all-to-all-done.2
  86.1 0.1 convert_reduce_fusion
  86.2 2.0 %collective-permute-start.2 = (f32[32,128]{1,0:T(8,128)S(1)}, f32[32,128]{1,0:T(8,128)S(1)}, u32[]{:S(2)}, u32[]{:S(2)}) collective-permute-start(f32[32,128]{1,0:T(8,128)S(1)} %convert_reduce_fusion), channel_id=1, source_target_pairs={{0,1},{1,0},{2,3},{3,2},{4,5},{5,4},{6,7},{7,6},{8,9},{9,8},{10,11... | collective-permute-start | bytes 49160 | tf_op jit(solution)/shard_map/sums/ppermute | solution.py:224
  88.2 0.0 collective-permute-done.8
  88.2 0.7 maximum_select_fusion
  88.9 0.1 collective-permute-done.2
  89.0 0.6 fusion
  (6 shorter events, 0.1 us)
Async XLA Ops:
  0.6 0.8 copy-start.1
  20.5 4.8 %copy-start.3 = (bf16[32,1728]{1,0:T(8,128)(2,1)S(1)}, bf16[32,1728]{1,0:T(8,128)(2,1)}, u32[]{:S(2)}) copy-start(bf16[32,1728]{1,0:T(8,128)(2,1)} %param.7) | copy-start | bytes 331780
  20.5 18.7 %all-to-all-start.1 = ((bf16[8,224,256]{2,1,0:T(8,128)(2,1)}), bf16[8,224,256]{2,1,0:T(8,128)(2,1)S(1)}, u32[]{:S(2)}, u32[]{:S(2)}) async-start(bf16[8,224,256]{2,1,0:T(8,128)(2,1)} %maximum_maximum_fusion), calls=%async_computation.1 | async-start | bytes 1835008 | tf_op jit(solution)/shard_map/strip/all_to_all | solution.py:247
  26.2 1.0 %copy-start.2 = (bf16[32,2,4096]{2,1,0:T(2,128)(2,1)S(1)}, bf16[32,2,4096]{2,1,0:T(2,128)(2,1)}, u32[]{:S(2)}) copy-start(bf16[32,2,4096]{2,1,0:T(2,128)(2,1)} %param.8) | copy-start | bytes 1572868
  26.5 1.1 %copy-start = (bf16[8,256,128]{2,1,0:T(8,128)(2,1)S(1)}, bf16[8,256,128]{2,1,0:T(8,128)(2,1)}, u32[]{:S(2)}) copy-start(bf16[8,256,128]{2,1,0:T(8,128)(2,1)} %constant.12.clone.taps_ref) | copy-start | bytes 1572868
  26.6 1.1 %copy-start.4 = (bf16[64,108]{1,0:T(8,128)(2,1)S(1)}, bf16[64,108]{1,0:T(8,128)(2,1)}, u32[]{:S(2)}) copy-start(bf16[64,108]{1,0:T(8,128)(2,1)} %param.6) | copy-start | bytes 41476
  39.2 3.6 %collective-permute-start = (bf16[8,224,256]{2,1,0:T(8,128)(2,1)S(1)}, bf16[8,224,256]{2,1,0:T(8,128)(2,1)}, u32[]{:S(2)}, u32[]{:S(2)}) collective-permute-start(bf16[8,224,256]{2,1,0:T(8,128)(2,1)S(1)} %all-to-all-done.1.own_ref), channel_id=1, source_target_pairs={{0,1},{1,0},{2,3},{3,2},{4,5},{5,4},{6,7},{7,6},{8,9},{9,8},{10,11... | collective-permute-start | bytes 2752520 | tf_op jit(solution)/shard_map/ppermute | solution.py:224
  65.2 1.4 %collective-permute-start.3 = (f32[16,1728]{1,0:T(8,128)S(1)}, f32[16,1728]{1,0:T(8,128)S(1)}, u32[]{:S(2)}, u32[]{:S(2)}) collective-permute-start(f32[16,1728]{1,0:T(8,128)S(1)} %get-tuple-element.26), channel_id=1, source_target_pairs={{0,1},{1,0},{2,3},{3,2},{4,5},{5,4},{6,7},{7,6},{8,9},{9,8},{10,11... | collective-permute-start | bytes 331784 | tf_op jit(solution)/shard_map/sums/ppermute | solution.py:224
  65.6 1.3 %collective-permute-start.1 = (f32[32,128]{1,0:T(8,128)S(1)}, f32[32,128]{1,0:T(8,128)S(1)}, u32[]{:S(2)}, u32[]{:S(2)}) collective-permute-start(f32[32,128]{1,0:T(8,128)S(1)} %get-tuple-element.21), channel_id=1, source_target_pairs={{0,1},{1,0},{2,3},{3,2},{4,5},{5,4},{6,7},{7,6},{8,9},{9,8},{10,11... | collective-permute-start | bytes 49160 | tf_op jit(solution)/shard_map/sums/ppermute | solution.py:224
  66.6 7.3 %collective-permute-start.4 = (bf16[16,1728]{1,0:T(8,128)(2,1)S(1)}, bf16[16,1728]{1,0:T(8,128)(2,1)S(1)}, u32[]{:S(2)}, u32[]{:S(2)}) collective-permute-start(bf16[16,1728]{1,0:T(8,128)(2,1)S(1)} %add_convert_fusion.1), channel_id=1, source_target_pairs={{0,8},{8,0},{1,9},{9,1},{2,10},{10,2},{3,11},{11,3},{4,12},{12,4},... | collective-permute-start | bytes 165896 | tf_op jit(solution)/shard_map/sums/ppermute | solution.py:272
  67.9 18.3 %all-to-all-start.2 = ((bf16[64,32,128]{2,1,0:T(8,128)(2,1)}), bf16[64,32,128]{2,1,0:T(8,128)(2,1)S(1)}, u32[]{:S(2)}, u32[]{:S(2)}) async-start(bf16[64,32,128]{2,1,0:T(8,128)(2,1)} %broadcast_in_dim.2), calls=%async_computation.2 | async-start | bytes 1048576 | tf_op jit(solution)/shard_map/sums/all_to_all | solution.py:264
  74.0 6.6 %collective-permute-start.5 = (bf16[16,1728]{1,0:T(8,128)(2,1)S(1)}, bf16[16,1728]{1,0:T(8,128)(2,1)S(1)}, u32[]{:S(2)}, u32[]{:S(2)}) collective-permute-start(bf16[16,1728]{1,0:T(8,128)(2,1)S(1)} %add_convert_fusion), channel_id=1, source_target_pairs={{0,4},{2,6},{4,0},{6,2},{1,5},{3,7},{5,1},{7,3},{8,12},{10,14},{12... | collective-permute-start | bytes 165896 | tf_op jit(solution)/shard_map/sums/ppermute | solution.py:273
  76.6 8.8 %collective-permute-start.6 = (bf16[16,1728]{1,0:T(8,128)(2,1)S(1)}, bf16[16,1728]{1,0:T(8,128)(2,1)S(1)}, u32[]{:S(2)}, u32[]{:S(2)}) collective-permute-start(bf16[16,1728]{1,0:T(8,128)(2,1)S(1)} %add_convert_fusion), channel_id=1, source_target_pairs={{0,2},{2,4},{4,6},{6,0},{1,3},{3,5},{5,7},{7,1},{8,10},{10,12},{12... | collective-permute-start | bytes 165896 | tf_op jit(solution)/shard_map/sums/ppermute | solution.py:273
  76.8 8.6 %collective-permute-start.7 = (bf16[16,1728]{1,0:T(8,128)(2,1)S(1)}, bf16[16,1728]{1,0:T(8,128)(2,1)S(1)}, u32[]{:S(2)}, u32[]{:S(2)}) collective-permute-start(bf16[16,1728]{1,0:T(8,128)(2,1)S(1)} %add_convert_fusion), channel_id=1, source_target_pairs={{0,6},{2,0},{4,2},{6,4},{1,7},{3,1},{5,3},{7,5},{8,14},{10,8},{12,... | collective-permute-start | bytes 165896 | tf_op jit(solution)/shard_map/sums/ppermute | solution.py:273
  85.4 2.8 %collective-permute-start.8 = (f32[16,1728]{1,0:T(8,128)S(1)}, f32[16,1728]{1,0:T(8,128)S(1)}, u32[]{:S(2)}, u32[]{:S(2)}) collective-permute-start(f32[16,1728]{1,0:T(8,128)S(1)} %convert_add_fusion), channel_id=1, source_target_pairs={{0,1},{1,0},{2,3},{3,2},{4,5},{5,4},{6,7},{7,6},{8,9},{9,8},{10,11... | collective-permute-start | bytes 331784 | tf_op jit(solution)/shard_map/sums/ppermute | solution.py:224
  86.2 2.8 %collective-permute-start.2 = (f32[32,128]{1,0:T(8,128)S(1)}, f32[32,128]{1,0:T(8,128)S(1)}, u32[]{:S(2)}, u32[]{:S(2)}) collective-permute-start(f32[32,128]{1,0:T(8,128)S(1)} %convert_reduce_fusion), channel_id=1, source_target_pairs={{0,1},{1,0},{2,3},{3,2},{4,5},{5,4},{6,7},{7,6},{8,9},{9,8},{10,11... | collective-permute-start | bytes 49160 | tf_op jit(solution)/shard_map/sums/ppermute | solution.py:224
